TPU v7x, 32 devices: a whole 2x2x4 slice. The times are simulated.
32 devices in a mesh: grp: 4 (over x, core), row: 4 (over z), col: 2 (over y).
Axes of the slice: x: 2, y: 2, z: 4, core: 2. Of those that a mesh axis runs over, the one named last changes fastest.
Arguments:
- tokens_in: bfloat16 [256, 6144], P('col', 'row'), may hold values from -6 to 6
- cotangent: bfloat16 [256, 6144], P('col', 'grp'), may hold values from -6 to 6
- sample_rows: int32 [64], P('col'), may hold values from 0 to 255, as said below
- act_inverse: bfloat16 [6144, 6144], P('grp', 'row'), as said below
- grad_inverse: bfloat16 [6144, 6144], P('grp', 'col'), as said below
Outputs:
- precond: float32 [6144, 6144], P(('grp', 'row'), 'col')
- act_cov: float32 [6144, 6144], P(('row', 'col'), 'grp')
- grad_cov: float32 [6144, 6144], P(('row', 'col'), 'grp')
Inputs may be any that keep to these rules, and one draw needn't show every extreme that they name: `sample_rows`: for each block c, entries c * 32 to (c + 1) * 32 - 1 are distinct token rows of that block, between c * 128 and (c + 1) * 128 - 1. `act_inverse`: Symmetric. `grad_inverse`: Symmetric.
All inputs are finite; a program needn't handle non-finite values.
Results may differ from a plain program's by a relative error of at most 0.03.
Values may be sent and summed in bfloat16 or wider, within the bound.
A program may use at most 128 MiB of HBM per device.

v0:
```python
import jax
import jax.numpy as jnp
from jax import lax
from jax.sharding import PartitionSpec as P


def body(tokens_in, cotangent, sample_rows, act_inverse, grad_inverse):
    feat_row = tokens_in.shape[1]
    feat_grp = cotangent.shape[1]
    n_row = lax.axis_size("row")
    n_col = lax.axis_size("col")
    n_grp = lax.axis_size("grp")
    width = feat_row * n_row
    contract = (((0,), (0,)), ((), ()))
    term = lax.dot_general(tokens_in, cotangent, contract, preferred_element_type=jnp.float32)
    summed = lax.psum(term.astype(jnp.bfloat16), "col")
    part_right = jnp.dot(summed, grad_inverse, preferred_element_type=jnp.float32)
    right = lax.psum(part_right.astype(jnp.bfloat16), "grp")
    precond = lax.psum_scatter(
        jnp.dot(act_inverse, right, preferred_element_type=jnp.float32).astype(jnp.bfloat16),
        "row",
        scatter_dimension=0,
        tiled=True,
    ).astype(jnp.float32)
    col_index = lax.axis_index("col")
    grp_index = lax.axis_index("grp")
    offsets = sample_rows - col_index * tokens_in.shape[0]
    picked_x = jnp.take(tokens_in, offsets, axis=0)
    picked_g = jnp.take(cotangent, offsets, axis=0)
    samples = picked_x.shape[0]
    total = samples * n_col
    act_panel = lax.all_gather(picked_x[None], ("row", "col"), axis=0, tiled=True).reshape(
        n_row, total, feat_row
    )
    grad_panel = lax.all_gather(picked_g[None], ("grp", "col"), axis=0, tiled=True).reshape(
        n_grp, total, feat_grp
    )
    tile = width // (n_row * n_col)
    first = (lax.axis_index("row") * n_col + col_index) * tile
    act_left = lax.dynamic_slice(
        act_panel, (first // feat_row, 0, first % feat_row), (1, total, tile)
    )[0]
    per = feat_grp // feat_row
    act_span = lax.dynamic_slice_in_dim(act_panel, grp_index * per, per, 0)
    act_cov = jnp.einsum("sa,psf->apf", act_left, act_span, preferred_element_type=jnp.float32)
    act_cov = act_cov.reshape(tile, feat_grp) / total
    grad_left = lax.dynamic_slice(
        grad_panel, (first // feat_grp, 0, first % feat_grp), (1, total, tile)
    )[0]
    grad_span = lax.dynamic_index_in_dim(grad_panel, grp_index, 0, keepdims=False)
    grad_cov = (
        lax.dot_general(grad_left, grad_span, contract, preferred_element_type=jnp.float32) / total
    )
    return (precond, act_cov, grad_cov)


def solution(mesh):
    return jax.shard_map(
        body,
        mesh=mesh,
        in_specs=(P("col", "row"), P("col", "grp"), P("col"), P("grp", "row"), P("grp", "col")),
        out_specs=(P(("grp", "row"), "col"), P(("row", "col"), "grp"), P(("row", "col"), "grp")),
        check_vma=False,
    )
```

profile of v0, /device:TPU:0, one launch (start us, length us, event | category | flops | bytes accessed | tf_op | source)
XLA Modules:
  0.0 539.6 jit_solution(12733729645069797671)
XLA Ops:
  7.2 0.0 copy-start
  7.2 0.0 all-reduce.3.cloned.1.call-start
  7.2 0.9 copy-done
  8.2 4.6 convolution_convert_fusion.2
  12.8 0.0 all-reduce.3.cloned.1.call-update
  12.8 0.0 all-reduce.5.cloned.1.call-start
  12.8 122.0 %all-reduce.3.cloned.1.call-done = bf16[1536,1536]{1,0:T(8,128)(2,1)} async-done(((bf16[1536,1536]{1,0:T(8,128)(2,1)}), bf16[1536,1536]{1,0:T(8,128)(2,1)}) %all-reduce.3.cloned.1.call-update) | async-done | bytes 4718608 | tf_op jit(solution)/shard_map/psum | solution.py:16
  134.8 20.2 %convolution_convert_fusion.1 = bf16[1536,3072]{1,0:T(8,128)(2,1)} fusion(bf16[1536,1536]{1,0:T(8,128)(2,1)} %all-reduce.3.cloned.1.call-done, bf16[1536,3072]{1,0:T(8,128)(2,1)} %param.11), kind=kOutput, calls=%fused_computation.3 | convolution fusion | flops 14500233216 | bytes 23592960 | tf_op jit(solution)/shard_map/dot_general | solution.py:17
  155.1 0.0 all-reduce.5.cloned.1.call-update
  155.1 0.0 reduce-scatter.4.cloned.1.call-start
  155.2 169.9 %all-reduce.5.cloned.1.call-done = bf16[1536,3072]{1,0:T(8,128)(2,1)} async-done(((bf16[1536,3072]{1,0:T(8,128)(2,1)}), bf16[1536,3072]{1,0:T(8,128)(2,1)}) %all-reduce.5.cloned.1.call-update) | async-done | bytes 9437200 | tf_op jit(solution)/shard_map/psum | solution.py:18
  325.1 20.3 %fusion = bf16[1536,3072]{0,1:T(8,128)(2,1)} fusion(bf16[1536,3072]{1,0:T(8,128)(2,1)} %all-reduce.5.cloned.1.call-done, bf16[1536,1536]{1,0:T(8,128)(2,1)} %param.10), kind=kOutput, calls=%fused_computation.4 | convolution fusion | flops 14500233216 | bytes 23592960 | tf_op jit(solution)/shard_map/dot_general | solution.py:20
  345.3 12.7 %copy.10 = bf16[1536,3072]{1,0:T(8,128)(2,1)} copy(bf16[1536,3072]{0,1:T(8,128)(2,1)} %fusion) | data formatting | bytes 18874368
  358.0 0.0 copy-start.2
  358.0 0.0 copy-start.1
  358.0 0.0 reduce-scatter.4.cloned.1.call-update
  358.0 0.6 copy-done.2
  358.7 0.6 gather_fusion.1
  359.3 0.0 copy-done.1
  359.3 0.6 gather_fusion
  360.0 0.1 broadcast_select_fusion
  360.1 18.4 %all-gather.1 = bf16[256,1536]{1,0:T(8,128)(2,1)S(1)} all-gather(bf16[32,1536]{1,0:T(8,128)(2,1)S(1)} %get-tuple-element.12), channel_id=3, replica_groups=mesh['grp'=4,'row'=4,'col'=2] {'grp','col'}, dimensions={0}, use_global_device_ids=true | all-gather | bytes 884736 | tf_op jit(solution)/shard_map/all_gather | solution.py:35
  378.5 35.8 %all-gather = bf16[256,1536]{1,0:T(8,128)(2,1)S(1)} all-gather(bf16[32,1536]{1,0:T(8,128)(2,1)S(1)} %get-tuple-element.13), channel_id=2, replica_groups=mesh['grp'=4,'row'=4,'col'=2] {'row','col'}, dimensions={0}, use_global_device_ids=true | all-gather | bytes 884736 | tf_op jit(solution)/shard_map/all_gather | solution.py:32
  414.3 3.1 convolution_multiply_fusion.1
  417.3 3.1 convolution_multiply_fusion
  420.4 106.5 %reduce-scatter.4.cloned.1.call-done = bf16[384,3072]{1,0:T(8,128)(2,1)} async-done(((bf16[1536,3072]{1,0:T(8,128)(2,1)}), bf16[384,3072]{1,0:T(8,128)(2,1)}) %reduce-scatter.4.cloned.1.call-update) | async-done | bytes 2359312
  526.9 3.0 copy.11
  529.9 3.1 copy.9
  (2 shorter events, 0.0 us)
Async XLA Ops:
  7.2 1.0 copy-start
  7.2 127.7 %all-reduce.3.cloned.1.call-start = ((), (), s32[]{:S(2)}) async-start(), calls=%async_computation.1 | async-start | bytes 9437184 | tf_op jit(solution)/shard_map/psum | solution.py:16
  12.8 312.3 %all-reduce.5.cloned.1.call-start = ((), (), s32[]{:S(2)}) async-start(), calls=%async_computation.2 | async-start | bytes 18874368 | tf_op jit(solution)/shard_map/psum | solution.py:18
  155.1 371.8 %reduce-scatter.4.cloned.1.call-start = ((), (), s32[]{:S(2)}) async-start(), calls=%async_computation.3 | async-start | bytes 11796480
  358.0 0.7 copy-start.2
  358.0 1.3 copy-start.1
Sparse Core Ops, SparseCore 0:
  12.9 121.9 all-reduce.2
  155.2 169.7 all-reduce.4
  358.1 168.7 reduce-scatter.3
where the time goes:
time: 540 us
  waiting for transfers between devices  398 us (74%)
  blocking collectives  54.2 us (10%)
  matrix products  51.2 us (9%)
  local copies, waits for them, and re-layouts  21.7 us (4%)
  between operations  13.8 us (3%)
    psum x1, waiting for transfers between devices, body(): right = lax.psum(part_right.astype(jnp.bfloat16), 'grp')  170 us
    psum x1, waiting for transfers between devices, body(): summed = lax.psum(term.astype(jnp.bfloat16), 'col')  122 us
    unnamed x4, waiting for transfers between devices  107 us
    all_gather x1, blocking collectives, body(): lax.all_gather(picked_x[None], ('row', 'col'), axis=0, tiled=True)  35.8 us
    unnamed x9, local copies, waits for them, and re-layouts  20.4 us
    dot_general x1, matrix products, body(): jnp.dot(act_inverse, right, preferred_element_type=jnp.float32)  20.3 us
    dot_general x1, matrix products, body(): jnp.dot(summed, grad_inverse, preferred_element_type=jnp.float32)  20.2 us
    all_gather x1, blocking collectives, body(): lax.all_gather(picked_g[None], ('grp', 'col'), axis=0, tiled=True)  18.4 us
  transfers between devices with their start and end apart: 3, of which 3 were waited for; matrix products, arithmetic and copies ran while one was open for 1% of the time, Pallas kernels for 0%

commit v1 on v0

--- a/solution.py
+++ b/solution.py
@@ -2,6 +2,8 @@
 import jax.numpy as jnp
 from jax import lax
 from jax.sharding import PartitionSpec as P
+
+SHRINK = 2.0 ** -16
 
 
 def body(tokens_in, cotangent, sample_rows, act_inverse, grad_inverse):
@@ -12,18 +14,22 @@
     n_grp = lax.axis_size("grp")
     width = feat_row * n_row
     contract = (((0,), (0,)), ((), ()))
-    term = lax.dot_general(tokens_in, cotangent, contract, preferred_element_type=jnp.float32)
-    summed = lax.psum(term.astype(jnp.bfloat16), "col")
-    part_right = jnp.dot(summed, grad_inverse, preferred_element_type=jnp.float32)
-    right = lax.psum(part_right.astype(jnp.bfloat16), "grp")
-    precond = lax.psum_scatter(
-        jnp.dot(act_inverse, right, preferred_element_type=jnp.float32).astype(jnp.bfloat16),
-        "row",
-        scatter_dimension=0,
-        tiled=True,
-    ).astype(jnp.float32)
     col_index = lax.axis_index("col")
     grp_index = lax.axis_index("grp")
+    row_index = lax.axis_index("row")
+    small = tokens_in * jnp.asarray(SHRINK, tokens_in.dtype)
+    part_u = lax.dot_general(
+        small, act_inverse, (((1,), (1,)), ((), ())), preferred_element_type=jnp.float32
+    )
+    u = lax.psum_scatter(part_u.astype(jnp.bfloat16), "row", scatter_dimension=1, tiled=True)
+    u = lax.all_gather(u, "col", axis=0, tiled=True)
+    all_cot = lax.all_gather(cotangent, "col", axis=0, tiled=True)
+    share = grad_inverse.shape[1] // n_row
+    mine = lax.dynamic_slice_in_dim(grad_inverse, row_index * share, share, 1)
+    part_v = jnp.dot(all_cot, mine, preferred_element_type=jnp.float32)
+    v = lax.psum(part_v.astype(jnp.bfloat16), "grp")
+    v = lax.all_gather(v, "row", axis=1, tiled=True)
+    precond = lax.dot_general(u, v, contract, preferred_element_type=jnp.float32) * (1 / SHRINK)
     offsets = sample_rows - col_index * tokens_in.shape[0]
     picked_x = jnp.take(tokens_in, offsets, axis=0)
     picked_g = jnp.take(cotangent, offsets, axis=0)
@@ -36,7 +42,7 @@
         n_grp, total, feat_grp
     )
     tile = width // (n_row * n_col)
-    first = (lax.axis_index("row") * n_col + col_index) * tile
+    first = (row_index * n_col + col_index) * tile
     act_left = lax.dynamic_slice(
         act_panel, (first // feat_row, 0, first % feat_row), (1, total, tile)
     )[0]

time: 540 us -> 137 us (0.25)
  waiting for transfers between devices: 398 us -> 29.2 us
  matrix products: 51.2 us -> 17.8 us
  local copies, waits for them, and re-layouts: 21.7 us -> 3.21 us
  blocking collectives: 54.2 us -> 70.4 us
    psum x2 -> x1, waiting for transfers between devices: 292 us -> 29.1 us  [body(): v = lax.psum(part_v.astype(jnp.bfloat16), 'grp')]
    unnamed x4, waiting for transfers between devices: 107 us -> 0.05 us
    dot_general x3, matrix products: 45.1 us -> 11.7 us  [the longest x1 4.42 us: body(): lax.dot_general(u, v, contract, preferred_element_type=jnp.float32)]
    unnamed x9 -> x8, local copies, waits for them, and re-layouts: 20.4 us -> 1.94 us
    all_gather x0 -> x2, blocking collectives: none -> 18.4 us  [the longest x1 13.1 us: body(): all_cot = lax.all_gather(cotangent, 'col', axis=0, tiled=True)]
  transfers between devices with their start and end apart: 3 -> 3, of which waited for: 3 -> 1; matrix products, arithmetic and copies ran while one was open for 1% -> 10% of each run, Pallas kernels for 0% -> 0%
where the time goes in v1:
time: 137 us; the launch traced here: 136 us
  blocking collectives  70.4 us (51%)
  waiting for transfers between devices  29.2 us (21%)
  matrix products  17.8 us (13%)
  between operations  15.6 us (11%)
  local copies, waits for them, and re-layouts  3.21 us (2%)
    all_gather x1, blocking collectives, body(): lax.all_gather(picked_x[None], ('row', 'col'), axis=0, tiled=True)  34.3 us
    psum x1, waiting for transfers between devices, body(): v = lax.psum(part_v.astype(jnp.bfloat16), 'grp')  29.1 us
    all_gather x1, blocking collectives, body(): lax.all_gather(picked_g[None], ('grp', 'col'), axis=0, tiled=True)  17.7 us
    all_gather x1, blocking collectives, body(): all_cot = lax.all_gather(cotangent, 'col', axis=0, tiled=True)  13.1 us
    all_gather x1, blocking collectives, body(): u = lax.all_gather(u, 'col', axis=0, tiled=True)  5.29 us
    dot_general x1, matrix products, body(): lax.dot_general(u, v, contract, preferred_element_type=jnp.float32)  4.42 us
    dot_general x1, matrix products, body(): lax.dot_general(small, act_inverse, (((1,), (1,)), ((), ())), preferred_e...  4.01 us
    dot_general x1, matrix products, body(): part_v = jnp.dot(all_cot, mine, preferred_element_type=jnp.float32)  3.23 us
  transfers between devices with their start and end apart: 3, of which 1 were waited for; matrix products, arithmetic and copies ran while one was open for 10% of the time, Pallas kernels for 0%

profile of v1, /device:TPU:0, one launch (start us, length us, event | category | flops | bytes accessed | tf_op | source)
XLA Modules:
  0.0 136.4 jit_solution(5551305683615271738)
XLA Ops:
  8.0 0.0 copy-start.1
  8.0 0.0 all-reduce.2.cloned.1.call-start
  8.1 13.1 %all_gather.16 = bf16[256,1536]{1,0:T(8,128)(2,1)S(1)} all-gather(bf16[128,1536]{1,0:T(8,128)(2,1)} %param.8), channel_id=1, replica_groups=mesh['grp'=4,'row'=4,'col'=2] {'col'}, dimensions={0}, use_global_device_ids=true | all-gather | bytes 1179648 | tf_op jit(solution)/shard_map/all_gather | solution.py:26
  21.2 3.2 %fusion.5 = bf16[256,768]{0,1:T(8,128)(2,1)} fusion(bf16[256,1536]{1,0:T(8,128)(2,1)S(1)} %all_gather.16, bf16[1536,3072]{1,0:T(8,128)(2,1)} %param.11, s32[]{:T(128)S(6)} %select_n.37), kind=kOutput, calls=%fused_computation.9 | convolution fusion | flops 604176384 | bytes 3538948 | tf_op jit(solution)/shard_map/dot_general | solution.py:29
  24.4 0.0 copy-start.2
  24.4 0.0 copy-start
  24.4 0.0 all-reduce.2.cloned.1.call-update
  24.5 0.0 reduce-scatter.4.cloned.1.call-start
  24.5 0.0 copy-done.1
  24.5 4.0 %convolution_convert_fusion = bf16[128,1536]{1,0:T(8,128)(2,1)S(1)} fusion(bf16[1536,1536]{1,0:T(8,128)(2,1)} %param.10, bf16[128,1536]{1,0:T(8,128)(2,1)S(1)} %copy-done.1), kind=kOutput, calls=%fused_computation.5 | convolution fusion | flops 604372992 | bytes 5505024 | tf_op jit(solution)/shard_map/dot_general | solution.py:21
  28.5 0.9 copy.8
  29.5 0.0 reduce-scatter.4.cloned.1.call-update
  29.5 0.0 all-gather.4.cloned.1.call-start
  29.5 29.1 %all-reduce.2.cloned.1.call-done = bf16[256,768]{0,1:T(8,128)(2,1)} async-done(((bf16[256,768]{0,1:T(8,128)(2,1)}), bf16[256,768]{0,1:T(8,128)(2,1)}) %all-reduce.2.cloned.1.call-update) | async-done | bytes 393232 | tf_op jit(solution)/shard_map/psum | solution.py:30
  58.7 0.0 all-gather.4.cloned.1.call-update
  58.7 0.0 copy-done.2
  58.8 0.0 copy-done
  58.8 0.6 gather_fusion.1
  59.4 0.6 gather_fusion
  60.1 0.1 broadcast_select_fusion
  60.2 17.7 %all-gather.1 = bf16[256,1536]{1,0:T(8,128)(2,1)S(1)} all-gather(bf16[32,1536]{1,0:T(8,128)(2,1)S(1)} %get-tuple-element.6), channel_id=3, replica_groups=mesh['grp'=4,'row'=4,'col'=2] {'grp','col'}, dimensions={0}, use_global_device_ids=true | all-gather | bytes 884736 | tf_op jit(solution)/shard_map/all_gather | solution.py:41
  77.8 34.3 %all-gather = bf16[256,1536]{1,0:T(8,128)(2,1)S(1)} all-gather(bf16[32,1536]{1,0:T(8,128)(2,1)S(1)} %get-tuple-element.7), channel_id=2, replica_groups=mesh['grp'=4,'row'=4,'col'=2] {'row','col'}, dimensions={0}, use_global_device_ids=true | all-gather | bytes 884736 | tf_op jit(solution)/shard_map/all_gather | solution.py:38
  112.1 3.1 %convolution_multiply_fusion.2 = f32[768,1536]{1,0:T(8,128)} fusion(bf16[4,64,1536]{2,1,0:T(8,128)(2,1)S(1)} %bitcast.24, s32[]{:T(128)S(6)} %select_n.42, s32[]{:T(128)S(6)} %select_n.39, s32[]{:T(128)S(6)} %select_n.41), kind=kOutput, calls=%fused_computation.4 | convolution fusion | flops 152174592 | bytes 5013516 | tf_op jit(solution)/shard_map/sa,psf->apf/dot_general | solution.py:51
  115.2 3.1 %convolution_multiply_fusion.1 = f32[768,1536]{1,0:T(8,128)} fusion(bf16[4,64,1536]{2,1,0:T(8,128)(2,1)S(1)} %bitcast.23, s32[]{:T(128)S(6)} %select_n.42, s32[]{:T(128)S(6)} %select_n.39, s32[]{:T(128)S(6)} %select_n.41), kind=kOutput, calls=%fused_computation.3 | convolution fusion | flops 152174592 | bytes 5013516 | tf_op jit(solution)/shard_map/dot_general | solution.py:58
  118.3 0.0 reduce-scatter.4.cloned.1.call-done
  118.3 1.0 copy.9
  119.3 5.3 %all_gather.15 = bf16[256,384]{1,0:T(8,128)(2,1)S(1)} all-gather(bf16[128,384]{1,0:T(8,128)(2,1)S(1)} %copy.9), channel_id=1, replica_groups=mesh['grp'=4,'row'=4,'col'=2] {'col'}, dimensions={0}, use_global_device_ids=true | all-gather | bytes 294912 | tf_op jit(solution)/shard_map/all_gather | solution.py:25
  124.6 0.0 all-gather.4.cloned.1.call-done
  124.6 4.4 %convolution_multiply_fusion = f32[384,3072]{1,0:T(8,128)} fusion(bf16[256,384]{1,0:T(8,128)(2,1)S(1)} %all_gather.15, bf16[256,3072]{0,1:T(8,128)(2,1)} %all-gather.4.cloned.1.call-done), kind=kOutput, calls=%fused_computation.2 | convolution fusion | flops 605159424 | bytes 6488064 | tf_op jit(solution)/shard_map/dot_general | solution.py:32
  (2 shorter events, 0.0 us)
Async XLA Ops:
  8.0 16.5 %copy-start.1 = (bf16[128,1536]{1,0:T(8,128)(2,1)S(1)}, bf16[128,1536]{1,0:T(8,128)(2,1)}, u32[]{:S(2)}) copy-start(bf16[128,1536]{1,0:T(8,128)(2,1)} %param.7) | copy-start | bytes 1179652
  8.0 50.6 %all-reduce.2.cloned.1.call-start = ((), (), s32[]{:S(2)}) async-start(), calls=%async_computation.1 | async-start | bytes 786432 | tf_op jit(solution)/shard_map/psum | solution.py:30
  24.4 34.3 %copy-start.2 = (s32[32]{0:T(128)S(1)}, s32[32]{0:T(128)}, u32[]{:S(2)}) copy-start(s32[32]{0:T(128)} %param.9) | copy-start | bytes 388
  24.4 34.3 %copy-start = (bf16[128,1536]{1,0:T(8,128)(2,1)S(1)}, bf16[128,1536]{1,0:T(8,128)(2,1)}, u32[]{:S(2)}) copy-start(bf16[128,1536]{1,0:T(8,128)(2,1)} %param.8) | copy-start | bytes 1179652
  24.5 93.8 %reduce-scatter.4.cloned.1.call-start = ((), (), s32[]{:S(2)}) async-start(), calls=%async_computation.3 | async-start | bytes 491520
  29.5 95.1 %all-gather.4.cloned.1.call-start = ((), (), s32[]{:S(2)}) async-start(), calls=%async_computation.2 | async-start | bytes 1966080 | tf_op jit(solution)/shard_map/all_gather | solution.py:31
Sparse Core Ops, SparseCore 0:
  24.6 34.0 all-reduce.1
Sparse Core Ops, SparseCore 1:
  29.6 22.0 reduce-scatter.3
  58.8 41.4 all-gather.3

commit v2 on v1

--- a/solution.py
+++ b/solution.py
@@ -1,9 +1,385 @@
+import functools
+
 import jax
 import jax.numpy as jnp
 from jax import lax
+from jax.experimental import pallas as pl
+from jax.experimental.pallas import tpu as pltpu
 from jax.sharding import PartitionSpec as P
 
 SHRINK = 2.0 ** -16
+BF16 = jnp.bfloat16
+F32 = jnp.float32
+CONTRACT = (((0,), (0,)), ((), ()))
+
+
+def gather_kernel(
+    rows_ref, t_hbm, c_hbm, a_hbm, g_hbm,
+    u_out, v_out, xl_out, xs_out, yl_out, ys_out,
+    t_v, c_v, a_v, g_v, oh_v, px_v, q_v, r1_s, r1_r, r2_s, r2_r,
+    w_s, w_r, w_v, h_s, h_r, u_v, v_v, xl_v, xs_v, yl_v, ys_v,
+    load_sem, out_sem, send_sem, recv_sem,
+):
+    grp, z, c = lax.axis_index("grp"), lax.axis_index("row"), lax.axis_index("col")
+    x, k = grp // 2, grp % 2
+    oc, ok, ox = 1 - c, 1 - k, 1 - x
+    z1 = z + 1 - 2 * (z % 2)
+    z2 = (z + 2) % 4
+    z3 = (z1 + 2) % 4
+    to_y = {"col": oc}
+    to_k = {"grp": 2 * x + ok}
+    to_x = {"grp": 2 * ox + k}
+    to_xk = {"grp": 2 * ox + ok}
+    to_z1 = {"row": z1}
+    to_z2 = {"row": z2}
+    tok = t_v.shape[0]
+    feat = t_v.shape[1]
+    share = g_v.shape[1]
+    half = xl_v.shape[2]
+    out_rows = u_v.shape[2]
+    piece = tok // 4
+
+    names = {}
+
+    def copy(name, src, dst, where):
+        i = names.setdefault(name, len(names))
+        return pltpu.make_async_remote_copy(
+            src_ref=src, dst_ref=dst, send_sem=send_sem.at[i], recv_sem=recv_sem.at[i],
+            device_id=where, device_id_type=pl.DeviceIdType.MESH,
+        )
+
+    loads = [
+        pltpu.make_async_copy(c_hbm, c_v.at[c], load_sem.at[0]),
+        pltpu.make_async_copy(
+            g_hbm.at[:, pl.ds(pl.multiple_of(z * share, 128), share)], g_v, load_sem.at[1]
+        ),
+        pltpu.make_async_copy(t_hbm, t_v, load_sem.at[2]),
+        pltpu.make_async_copy(a_hbm, a_v, load_sem.at[3]),
+    ]
+    for load in loads:
+        load.start()
+
+    barrier = pltpu.get_barrier_semaphore()
+    partners = [to_y, to_k, to_x, to_xk, to_z1, to_z2]
+    for where in partners:
+        pl.semaphore_signal(barrier, inc=1, device_id=where, device_id_type=pl.DeviceIdType.MESH)
+    pl.semaphore_wait(barrier, len(partners))
+
+    cot = copy("cot", c_hbm, c_v.at[c], to_y)
+    cot_in = copy("cot", c_hbm, c_v.at[oc], to_y)
+    cot.start()
+
+    hot = (rows_ref[...] == lax.broadcasted_iota(jnp.int32, (rows_ref.shape[0], tok), 1))
+    hot = jnp.where(hot, 1.0, 0.0).astype(BF16)
+    oh_v[c] = hot
+    hot_out = copy("hot", oh_v.at[c], oh_v.at[c], to_y)
+    hot_in = copy("hot", oh_v.at[oc], oh_v.at[oc], to_y)
+    hot_out.start()
+    sends = [cot, hot_out]
+
+    def v_at(block, core, side, zz):
+        row = pl.multiple_of(block * tok + core * (2 * piece) + side * piece, piece)
+        return v_v.at[pl.ds(row, piece), pl.ds(pl.multiple_of(zz * share, 128), share)]
+
+    def send(name, src, dst, where):
+        out = copy(name, src, dst, where)
+        out.start()
+        sends.append(out)
+
+    def await_in(name, dst, where):
+        copy(name, dst, dst, where).wait_recv()
+
+    def product(ph, block):
+        q = jnp.dot(c_v[block], g_v[...], preferred_element_type=F32)
+        q_v[ph] = q.reshape(4, piece, share)
+        r1_s[ph] = q_v[ph, pl.ds(2 * ok, 2)].astype(BF16)
+        send(("r1", ph), r1_s.at[ph], r1_r.at[ph], to_k)
+
+    def across(ph):
+        await_in(("r1", ph), r1_r.at[ph], to_k)
+        r2_s[ph] = (q_v[ph, 2 * k + ox] + r1_r[ph, ox].astype(F32)).astype(BF16)
+        send(("r2", ph), r2_s.at[ph], r2_r.at[ph], to_x)
+
+    def finish(ph, block):
+        await_in(("r2", ph), r2_r.at[ph], to_x)
+        total = q_v[ph, 2 * k + x] + r1_r[ph, x].astype(F32) + r2_r[ph].astype(F32)
+        mine = v_at(block, k, x, z)
+        mine[...] = total.astype(BF16)
+        send(("v2", ph), mine, mine, to_z2)
+        send(("v1", ph), mine, mine, to_z1)
+        send(("vx", ph, 0), mine, mine, to_x)
+        send(("vk", ph, 0), mine, mine, to_k)
+
+    def spread(ph, block, step):
+        zz = (z, z2, z1, z3)[step]
+        got = v_at(block, k, x, zz)
+        await_in((("v0", "v2", "v1", "v3")[step], ph), got, to_z1)
+        if step == 1:
+            send(("v3", ph), got, got, to_z1)
+        send(("vx", ph, step), got, got, to_x)
+        send(("vk", ph, step), got, got, to_k)
+
+    def relay(ph, block, step):
+        zz = (z, z2, z1, z3)[step]
+        got = v_at(block, k, ox, zz)
+        await_in(("vx", ph, step), got, to_x)
+        send(("vk", ph, 4 + step), got, got, to_k)
+
+    def collect(ph, block):
+        for step in range(4):
+            zz = (z, z2, z1, z3)[step]
+            await_in(("vk", ph, step), v_at(block, ok, x, zz), to_k)
+        for step in range(4):
+            zz = (z, z2, z1, z3)[step]
+            await_in(("vk", ph, 4 + step), v_at(block, ok, ox, zz), to_k)
+
+    def u_part(block):
+        rows = a_v[pl.ds(pl.multiple_of(block * out_rows, out_rows), out_rows), :]
+        return lax.dot_general(t_v[...], rows, (((1,), (1,)), ((), ())), preferred_element_type=F32)
+
+    def at_half(ref, index):
+        return ref.at[:, pl.ds(pl.multiple_of(index * half, 128), half)]
+
+    loads[0].wait()
+    loads[1].wait()
+    product(0, c)
+
+    loads[2].wait()
+    px_v[...] = jnp.dot(hot, t_v[...], preferred_element_type=F32).astype(BF16)
+    send("xl", at_half(px_v, oc), xl_v.at[c], to_y)
+    xl_v[c] = at_half(px_v, c)[...]
+    has_span = grp == z
+    span = xs_v.at[c]
+
+    @pl.when(has_span)
+    def _():
+        xs_v[c] = px_v[...]
+
+    x_z2 = copy("x2", span, span, to_z2)
+    x_z1 = copy("x1", span, span, to_z1)
+    x_y = copy("xy", span, span, to_y)
+
+    @pl.when(has_span)
+    def _():
+        x_z2.start()
+        x_z1.start()
+
+    ys_v[c] = jnp.dot(hot, c_v[c], preferred_element_type=F32).astype(BF16)
+    across(0)
+
+    t_v[...] = t_v[...] * jnp.asarray(SHRINK, BF16)
+    loads[3].wait()
+    other = 1 - z % 2
+    for i in range(2):
+        w_s[i] = u_part(other + 2 * i).astype(BF16)
+    send("w", w_s, w_r, to_z1)
+    finish(0, c)
+    for i in range(2):
+        w_v[i] = u_part(z % 2 + 2 * i)
+
+    is_z2 = grp == z2
+    is_z1 = grp == z1
+
+    @pl.when(is_z2)
+    def _():
+        x_z2.wait_recv()
+        x_z1.start()
+
+    await_in("w", w_r, to_z1)
+    mine, away = z // 2, 1 - z // 2
+    h_s[...] = (w_v[away] + w_r[away].astype(F32)).astype(BF16)
+    send("h", h_s, h_r, to_z2)
+    spread(0, c, 1)
+    spread(0, c, 2)
+
+    @pl.when(jnp.logical_or(is_z1, grp == z3))
+    def _():
+        x_z1.wait_recv()
+
+    x_y.start()
+    sends.append(x_y)
+    await_in("h", h_r, to_z2)
+    u_v[c] = (w_v[mine] + w_r[mine].astype(F32) + h_r[...].astype(F32)).astype(BF16)
+    send("u", u_v.at[c], u_v.at[c], to_y)
+    spread(0, c, 3)
+
+    cot_in.wait_recv()
+    product(1, oc)
+    hot_in.wait_recv()
+    ys_v[oc] = jnp.dot(oh_v[oc], c_v[oc], preferred_element_type=F32).astype(BF16)
+    left = ys_v.at[:, :, pl.ds(pl.multiple_of(c * half, 128), half)]
+    y_outs = [copy(("yl", i), left, yl_v, w) for i, w in enumerate([to_k, to_x, to_xk])]
+
+    @pl.when(has_span)
+    def _():
+        for out in y_outs:
+            out.start()
+        yl_v[...] = left[...]
+
+    across(1)
+    for step in range(4):
+        relay(0, c, step)
+    finish(1, oc)
+    for step in range(1, 4):
+        spread(1, oc, step)
+    collect(0, c)
+
+    outs = [pltpu.make_async_copy(
+        v_v.at[pl.ds(pl.multiple_of(c * tok, tok), tok)],
+        v_out.at[pl.ds(pl.multiple_of(c * tok, tok), tok)], out_sem.at[0])]
+    outs[0].start()
+    await_in("xl", xl_v.at[oc], to_y)
+    await_in("xy", xs_v.at[oc], to_y)
+    await_in("u", u_v.at[oc], to_y)
+    for i, (src, dst) in enumerate([(u_v, u_out), (xl_v, xl_out), (xs_v, xs_out), (ys_v, ys_out)]):
+        out = pltpu.make_async_copy(src, dst, out_sem.at[2 + i])
+        out.start()
+        outs.append(out)
+
+    @pl.when(grp == 2 * (z // 2) + (1 - z % 2))
+    def _():
+        y_outs[0].wait_recv()
+
+    @pl.when(grp == 2 * (1 - z // 2) + z % 2)
+    def _():
+        y_outs[1].wait_recv()
+
+    @pl.when(grp == 2 * (1 - z // 2) + (1 - z % 2))
+    def _():
+        y_outs[2].wait_recv()
+
+    out = pltpu.make_async_copy(yl_v, yl_out, out_sem.at[6])
+    out.start()
+    outs.append(out)
+    for step in range(4):
+        relay(1, oc, step)
+    collect(1, oc)
+    out = pltpu.make_async_copy(
+        v_v.at[pl.ds(pl.multiple_of(oc * tok, tok), tok)],
+        v_out.at[pl.ds(pl.multiple_of(oc * tok, tok), tok)], out_sem.at[1])
+    out.start()
+    outs.append(out)
+
+    @pl.when(has_span)
+    def _():
+        x_z2.wait_send()
+        x_z1.wait_send()
+        for out in y_outs:
+            out.wait_send()
+
+    @pl.when(is_z2)
+    def _():
+        x_z1.wait_send()
+
+    for out in sends:
+        out.wait_send()
+    for out in outs:
+        out.wait()
+
+
+def gather(rows, tokens_in, cotangent, act_inverse, grad_inverse, n_row):
+    tok, feat = tokens_in.shape
+    samples = rows.shape[0]
+    share = grad_inverse.shape[1] // n_row
+    out_rows = feat // n_row
+    half = feat // 2
+    piece = tok // 4
+    shapes = [
+        (2, tok, out_rows), (2 * tok, grad_inverse.shape[1]),
+        (2, samples, half), (2, samples, feat), (2, samples, half), (2, samples, feat),
+    ]
+    vmem = pltpu.VMEM
+    return pl.pallas_call(
+        gather_kernel,
+        out_shape=[jax.ShapeDtypeStruct(s, BF16) for s in shapes],
+        in_specs=[pl.BlockSpec(memory_space=vmem)] + [pl.BlockSpec(memory_space=pl.ANY)] * 4,
+        out_specs=[pl.BlockSpec(memory_space=pl.ANY)] * 6,
+        scratch_shapes=[
+            vmem((tok, feat), BF16),
+            vmem((2, tok, feat), BF16),
+            vmem(act_inverse.shape, BF16),
+            vmem((feat, share), BF16),
+            vmem((2, samples, tok), BF16),
+            vmem((samples, feat), BF16),
+            vmem((2, 4, piece, share), F32),
+            vmem((2, 2, piece, share), BF16),
+            vmem((2, 2, piece, share), BF16),
+            vmem((2, piece, share), BF16),
+            vmem((2, piece, share), BF16),
+            vmem((2, tok, out_rows), BF16),
+            vmem((2, tok, out_rows), BF16),
+            vmem((2, tok, out_rows), F32),
+            vmem((tok, out_rows), BF16),
+            vmem((tok, out_rows), BF16),
+        ] + [vmem(s, BF16) for s in shapes] + [
+            pltpu.SemaphoreType.DMA((4,)),
+            pltpu.SemaphoreType.DMA((7,)),
+            pltpu.SemaphoreType.DMA((48,)),
+            pltpu.SemaphoreType.DMA((48,)),
+        ],
+        compiler_params=pltpu.CompilerParams(
+            collective_id=0, has_side_effects=True, vmem_limit_bytes=40 * 2 ** 20
+        ),
+        cost_estimate=pl.CostEstimate(flops=3 * 10 ** 9, bytes_accessed=10 ** 7, transcendentals=0),
+    )(rows, tokens_in, cotangent, act_inverse, grad_inverse)
+
+
+def product_kernel(total, u, v, xl, xs, yl, ys, p_out, a_out, g_out, ut, xt, yt):
+    @pl.when(pl.program_id(0) == 0)
+    def _():
+        ut[...] = u[...].T
+        xt[...] = xl[...].T
+        yt[...] = yl[...].T
+
+    a_out[...] = jnp.dot(xt[...], xs[...], preferred_element_type=F32) * (1 / total)
+    g_out[...] = jnp.dot(yt[...], ys[...], preferred_element_type=F32) * (1 / total)
+    p_out[...] = jnp.dot(ut[...], v[...], preferred_element_type=F32) * (1 / SHRINK)
+
+
+def products(u, v, xl, xs, yl, ys):
+    steps = 6
+    total = xl.shape[0]
+
+    def whole(a):
+        return pl.BlockSpec(a.shape, lambda i: (0, 0))
+
+    def cut(rows, width):
+        return pl.BlockSpec((rows, width // steps), lambda i: (0, i))
+
+    return pl.pallas_call(
+        functools.partial(product_kernel, total),
+        grid=(steps,),
+        in_specs=[
+            whole(u), cut(v.shape[0], v.shape[1]),
+            whole(xl), cut(total, xs.shape[1]), whole(yl), cut(total, ys.shape[1]),
+        ],
+        out_specs=[
+            cut(u.shape[1], v.shape[1]), cut(xl.shape[1], xs.shape[1]), cut(yl.shape[1], ys.shape[1])
+        ],
+        out_shape=[
+            jax.ShapeDtypeStruct((u.shape[1], v.shape[1]), F32),
+            jax.ShapeDtypeStruct((xl.shape[1], xs.shape[1]), F32),
+            jax.ShapeDtypeStruct((yl.shape[1], ys.shape[1]), F32),
+        ],
+        scratch_shapes=[
+            pltpu.VMEM(u.shape[::-1], BF16), pltpu.VMEM(xl.shape[::-1], BF16),
+            pltpu.VMEM(yl.shape[::-1], BF16),
+        ],
+        compiler_params=pltpu.CompilerParams(vmem_limit_bytes=40 * 2 ** 20),
+        cost_estimate=pl.CostEstimate(flops=10 ** 9, bytes_accessed=17 * 10 ** 6, transcendentals=0),
+    )(u, v, xl, xs, yl, ys)
+
+
+def flat(a):
+    return a.reshape(-1, a.shape[-1])
+
+
+def body_kernels(tokens_in, cotangent, sample_rows, act_inverse, grad_inverse):
+    rows = (sample_rows - lax.axis_index("col") * tokens_in.shape[0])[:, None]
+    u, v, xl, xs, yl, ys = gather(
+        rows, tokens_in, cotangent, act_inverse, grad_inverse, lax.axis_size("row")
+    )
+    return tuple(products(flat(u), v, flat(xl), flat(xs), flat(yl), flat(ys)))
 
 
 def body(tokens_in, cotangent, sample_rows, act_inverse, grad_inverse):
@@ -61,8 +437,9 @@
 
 
 def solution(mesh):
+    sizes = tuple(mesh.shape[name] for name in ("grp", "row", "col"))
     return jax.shard_map(
-        body,
+        body_kernels if sizes == (4, 4, 2) else body,
         mesh=mesh,
         in_specs=(P("col", "row"), P("col", "grp"), P("col"), P("grp", "row"), P("grp", "col")),
         out_specs=(P(("grp", "row"), "col"), P(("row", "col"), "grp"), P(("row", "col"), "grp")),

time: 137 us -> 50.6 us (0.37)
  the two profiles are of different devices: /device:TPU:0 before, /device:TPU:11 now
where the time goes in v2:
time: 50.6 us; the launch traced here: 50.3 us
  Pallas kernels  44.6 us (88%)
  local copies, waits for them, and re-layouts  4.42 us (9%)
  other arithmetic  0.66 us (1%)
  between operations  0.65 us (1%)
    pallas_call x1, Pallas kernels, gather(): pl.pallas_call(gather_kernel, out_shape=[jax.ShapeDtypeStruct(s, BF16) fo...  38.3 us
    pallas_call x1, Pallas kernels, products(): pl.pallas_call(functools.partial(product_kernel, total), grid=(steps,), i...  6.27 us
    unnamed x6, local copies, waits for them, and re-layouts  4.33 us

profile of v2, /device:TPU:11, one launch (start us, length us, event | category | flops | bytes accessed | tf_op | source)
XLA Modules:
  0.0 50.3 jit_solution(16349258796183687140)
XLA Ops:
  0.6 0.7 %subtract_bitcast_fusion = s32[32,1]{0,1:T(1,128)S(1)} fusion(s32[32]{0:T(128)} %param.7, s32[]{:T(128)S(6)} %mul.3), kind=kLoop, calls=%fused_computation | loop fusion | flops 32 | bytes 260 | tf_op jit(solution)/shard_map/broadcast_in_dim | solution.py:378
  1.3 0.1 copy.8.rows_ref
  1.4 0.0 copy-start
  1.4 2.3 %copy-done = bf16[1536,1536]{1,0:T(8,128)(2,1)S(1)} copy-done((bf16[1536,1536]{1,0:T(8,128)(2,1)S(1)}, bf16[1536,1536]{1,0:T(8,128)(2,1)}, u32[]{:S(2)}) %copy-start) | copy-done | bytes 4718616
  3.7 0.0 copy-start.1
  3.7 1.0 %copy-done.1 = bf16[128,1536]{1,0:T(8,128)(2,1)S(1)} copy-done((bf16[128,1536]{1,0:T(8,128)(2,1)S(1)}, bf16[128,1536]{1,0:T(8,128)(2,1)}, u32[]{:S(2)}) %copy-start.1) | copy-done | bytes 393240
  4.7 0.0 copy-start.2
  4.7 1.0 %copy-done.2 = bf16[128,1536]{1,0:T(8,128)(2,1)S(1)} copy-done((bf16[128,1536]{1,0:T(8,128)(2,1)S(1)}, bf16[128,1536]{1,0:T(8,128)(2,1)}, u32[]{:S(2)}) %copy-start.2) | copy-done | bytes 393240
  5.7 38.3 %shard_map.76 = (bf16[2,128,384]{2,1,0:T(8,128)(2,1)S(1)}, bf16[256,3072]{1,0:T(8,128)(2,1)S(1)}, bf16[2,32,768]{2,1,0:T(8,128)(2,1)S(1)}, bf16[2,32,1536]{2,1,0...) custom-call(s32[32,1]{1,0:T(8,128)S(1)} %copy.8.rows_ref, ...), custom_call_target="tpu_custom_call" | custom-call | flops 3000000000 | bytes 10000000 | tf_op jit(solution)/shard_map/pallas_call | solution.py:292
  44.1 6.3 %shard_map.77 = (f32[384,3072]{1,0:T(8,128)}, f32[768,1536]{1,0:T(8,128)}, f32[768,1536]{1,0:T(8,128)}) custom-call(bf16[256,384]{1,0:T(8,128)(2,1)S(1)} %bitcast.7, bf16[256,3072]{1,0:T(8,128)(2,1)S(1)} %get-tuple-element.10.v, bf16[64,768]{1,0:T(8,128)(2,1)S(1)} %bitcast.10, bf16[64,1536]{1,0:T(8,128)(2,1)S(1)} %bitcast.8, bf16[64,768]{1,0:T(8,128)(2,1)S(1)} %bitcast.11, ...), custom_call_target="tpu_custom_call" | custom-call | flops 1000000000 | bytes 17000000 | tf_op jit(solution)/shard_map/pallas_call | solution.py:349
Async XLA Ops:
  1.4 2.3 %copy-start = (bf16[1536,1536]{1,0:T(8,128)(2,1)S(1)}, bf16[1536,1536]{1,0:T(8,128)(2,1)}, u32[]{:S(2)}) copy-start(bf16[1536,1536]{1,0:T(8,128)(2,1)} %a_hbm.1) | copy-start | bytes 14155780
  3.7 1.0 %copy-start.1 = (bf16[128,1536]{1,0:T(8,128)(2,1)S(1)}, bf16[128,1536]{1,0:T(8,128)(2,1)}, u32[]{:S(2)}) copy-start(bf16[128,1536]{1,0:T(8,128)(2,1)} %t_hbm.1) | copy-start | bytes 1179652
  4.7 1.0 %copy-start.2 = (bf16[128,1536]{1,0:T(8,128)(2,1)S(1)}, bf16[128,1536]{1,0:T(8,128)(2,1)}, u32[]{:S(2)}) copy-start(bf16[128,1536]{1,0:T(8,128)(2,1)} %c_hbm.1) | copy-start | bytes 1179652

commit v3 on v2

--- a/solution.py
+++ b/solution.py
@@ -26,6 +26,7 @@
     z1 = z + 1 - 2 * (z % 2)
     z2 = (z + 2) % 4
     z3 = (z1 + 2) % 4
+    places = (z, z2, z1, z3)
     to_y = {"col": oc}
     to_k = {"grp": 2 * x + ok}
     to_x = {"grp": 2 * ox + k}
@@ -33,13 +34,13 @@
     to_z1 = {"row": z1}
     to_z2 = {"row": z2}
     tok = t_v.shape[0]
-    feat = t_v.shape[1]
     share = g_v.shape[1]
     half = xl_v.shape[2]
     out_rows = u_v.shape[2]
-    piece = tok // 4
+    phases = ((c, 0, tok), (oc, 0, tok // 2), (oc, tok // 2, tok // 2))
 
     names = {}
+    sends = []
 
     def copy(name, src, dst, where):
         i = names.setdefault(name, len(names))
@@ -47,6 +48,14 @@
             src_ref=src, dst_ref=dst, send_sem=send_sem.at[i], recv_sem=recv_sem.at[i],
             device_id=where, device_id_type=pl.DeviceIdType.MESH,
         )
+
+    def send(name, src, dst, where):
+        out = copy(name, src, dst, where)
+        out.start()
+        sends.append(out)
+
+    def await_in(name, dst, where):
+        copy(name, dst, dst, where).wait_recv()
 
     loads = [
         pltpu.make_async_copy(c_hbm, c_v.at[c], load_sem.at[0]),
@@ -65,73 +74,72 @@
         pl.semaphore_signal(barrier, inc=1, device_id=where, device_id_type=pl.DeviceIdType.MESH)
     pl.semaphore_wait(barrier, len(partners))
 
-    cot = copy("cot", c_hbm, c_v.at[c], to_y)
-    cot_in = copy("cot", c_hbm, c_v.at[oc], to_y)
-    cot.start()
-
-    hot = (rows_ref[...] == lax.broadcasted_iota(jnp.int32, (rows_ref.shape[0], tok), 1))
-    hot = jnp.where(hot, 1.0, 0.0).astype(BF16)
-    oh_v[c] = hot
-    hot_out = copy("hot", oh_v.at[c], oh_v.at[c], to_y)
-    hot_in = copy("hot", oh_v.at[oc], oh_v.at[oc], to_y)
-    hot_out.start()
-    sends = [cot, hot_out]
-
-    def v_at(block, core, side, zz):
-        row = pl.multiple_of(block * tok + core * (2 * piece) + side * piece, piece)
-        return v_v.at[pl.ds(row, piece), pl.ds(pl.multiple_of(zz * share, 128), share)]
-
-    def send(name, src, dst, where):
-        out = copy(name, src, dst, where)
-        out.start()
-        sends.append(out)
-
-    def await_in(name, dst, where):
-        copy(name, dst, dst, where).wait_recv()
-
-    def product(ph, block):
-        q = jnp.dot(c_v[block], g_v[...], preferred_element_type=F32)
-        q_v[ph] = q.reshape(4, piece, share)
-        r1_s[ph] = q_v[ph, pl.ds(2 * ok, 2)].astype(BF16)
-        send(("r1", ph), r1_s.at[ph], r1_r.at[ph], to_k)
+    for ph in (1, 2):
+        part = pl.ds(phases[ph][1], phases[ph][2])
+        send(("cot", ph), c_hbm.at[part], c_v.at[c, part], to_y)
+
+    hot = lax.broadcasted_iota(jnp.int32, (tok, rows_ref.shape[1]), 0) + c * tok == rows_ref[...]
+    oh_v[c] = jnp.where(hot, 1.0, 0.0).astype(BF16)
+    send("hot", oh_v.at[c], oh_v.at[c], to_y)
+
+    def pick(block, values):
+        return lax.dot_general(oh_v[block], values, CONTRACT, preferred_element_type=F32).astype(BF16)
+
+    def v_at(ph, core, side, step):
+        block, first, count = phases[ph]
+        row = pl.multiple_of(block * tok + first + (2 * core + side) * (count // 4), count // 4)
+        return v_v.at[
+            pl.ds(row, count // 4), pl.ds(pl.multiple_of(places[step] * share, 128), share)
+        ]
+
+    def cut(ph):
+        return pl.ds(0, phases[ph][2] // 4)
+
+    def product(ph):
+        block, first, count = phases[ph]
+        q = jnp.dot(c_v[block, first:first + count], g_v[...], preferred_element_type=F32)
+        q_v[ph, :, cut(ph)] = q.reshape(4, count // 4, share)
+        r1_s[ph, :, cut(ph)] = q_v[ph, pl.ds(2 * ok, 2), cut(ph)].astype(BF16)
+        send(("r1", ph), r1_s.at[ph, :, cut(ph)], r1_r.at[ph, :, cut(ph)], to_k)
 
     def across(ph):
-        await_in(("r1", ph), r1_r.at[ph], to_k)
-        r2_s[ph] = (q_v[ph, 2 * k + ox] + r1_r[ph, ox].astype(F32)).astype(BF16)
-        send(("r2", ph), r2_s.at[ph], r2_r.at[ph], to_x)
-
-    def finish(ph, block):
-        await_in(("r2", ph), r2_r.at[ph], to_x)
-        total = q_v[ph, 2 * k + x] + r1_r[ph, x].astype(F32) + r2_r[ph].astype(F32)
-        mine = v_at(block, k, x, z)
+        await_in(("r1", ph), r1_r.at[ph, :, cut(ph)], to_k)
+        r2_s[ph, cut(ph)] = (
+            q_v[ph, 2 * k + ox, cut(ph)] + r1_r[ph, ox, cut(ph)].astype(F32)
+        ).astype(BF16)
+        send(("r2", ph), r2_s.at[ph, cut(ph)], r2_r.at[ph, cut(ph)], to_x)
+
+    def finish(ph):
+        await_in(("r2", ph), r2_r.at[ph, cut(ph)], to_x)
+        total = (
+            q_v[ph, 2 * k + x, cut(ph)] + r1_r[ph, x, cut(ph)].astype(F32)
+            + r2_r[ph, cut(ph)].astype(F32)
+        )
+        mine = v_at(ph, k, x, 0)
         mine[...] = total.astype(BF16)
-        send(("v2", ph), mine, mine, to_z2)
-        send(("v1", ph), mine, mine, to_z1)
+        send(("v", ph, 1), mine, mine, to_z2)
+        send(("v", ph, 2), mine, mine, to_z1)
         send(("vx", ph, 0), mine, mine, to_x)
         send(("vk", ph, 0), mine, mine, to_k)
 
-    def spread(ph, block, step):
-        zz = (z, z2, z1, z3)[step]
-        got = v_at(block, k, x, zz)
-        await_in((("v0", "v2", "v1", "v3")[step], ph), got, to_z1)
+    def spread(ph, step):
+        got = v_at(ph, k, x, step)
+        await_in(("v", ph, step), got, to_z1)
         if step == 1:
-            send(("v3", ph), got, got, to_z1)
+            send(("v", ph, 3), got, got, to_z1)
         send(("vx", ph, step), got, got, to_x)
         send(("vk", ph, step), got, got, to_k)
 
-    def relay(ph, block, step):
-        zz = (z, z2, z1, z3)[step]
-        got = v_at(block, k, ox, zz)
+    def relay(ph, step):
+        got = v_at(ph, k, ox, step)
         await_in(("vx", ph, step), got, to_x)
         send(("vk", ph, 4 + step), got, got, to_k)
 
-    def collect(ph, block):
+    def collect(ph):
         for step in range(4):
-            zz = (z, z2, z1, z3)[step]
-            await_in(("vk", ph, step), v_at(block, ok, x, zz), to_k)
+            await_in(("vk", ph, step), v_at(ph, ok, x, step), to_k)
         for step in range(4):
-            zz = (z, z2, z1, z3)[step]
-            await_in(("vk", ph, 4 + step), v_at(block, ok, ox, zz), to_k)
+            await_in(("vk", ph, 4 + step), v_at(ph, ok, ox, step), to_k)
 
     def u_part(block):
         rows = a_v[pl.ds(pl.multiple_of(block * out_rows, out_rows), out_rows), :]
@@ -140,102 +148,115 @@
     def at_half(ref, index):
         return ref.at[:, pl.ds(pl.multiple_of(index * half, 128), half)]
 
+    def await_cot(ph):
+        part = pl.ds(phases[ph][1], phases[ph][2])
+        await_in(("cot", ph), c_v.at[oc, part], to_y)
+
+    has_span = grp == z
+    is_z2 = grp == z2
+    is_z1 = grp == z1
+    span = xs_v.at[c]
+    x_z2 = copy("x2", span, span, to_z2)
+    x_z1 = copy("x1", span, span, to_z1)
+
     loads[0].wait()
     loads[1].wait()
-    product(0, c)
-
+    product(0)
     loads[2].wait()
-    px_v[...] = jnp.dot(hot, t_v[...], preferred_element_type=F32).astype(BF16)
+    px_v[...] = pick(c, t_v[...])
+    t_v[...] = t_v[...] * jnp.asarray(SHRINK, BF16)
+    ys_v[c] = pick(c, c_v[c])
+    across(0)
+
+    loads[3].wait()
+    for i in range(2):
+        w_s[i] = u_part(1 - z % 2 + 2 * i).astype(BF16)
+    send("w", w_s, w_r, to_z1)
+
+    @pl.when(has_span)
+    def _():
+        xs_v[c] = px_v[...]
+        x_z2.start()
+        x_z1.start()
+
+    finish(0)
+    await_cot(1)
+    product(1)
+    for i in range(2):
+        w_v[i] = u_part(z % 2 + 2 * i)
+    across(1)
+    finish(1)
+    spread(0, 1)
+    spread(0, 2)
+    await_cot(2)
+    product(2)
     send("xl", at_half(px_v, oc), xl_v.at[c], to_y)
     xl_v[c] = at_half(px_v, c)[...]
-    has_span = grp == z
-    span = xs_v.at[c]
-
-    @pl.when(has_span)
-    def _():
-        xs_v[c] = px_v[...]
-
-    x_z2 = copy("x2", span, span, to_z2)
-    x_z1 = copy("x1", span, span, to_z1)
-    x_y = copy("xy", span, span, to_y)
-
-    @pl.when(has_span)
-    def _():
-        x_z2.start()
-        x_z1.start()
-
-    ys_v[c] = jnp.dot(hot, c_v[c], preferred_element_type=F32).astype(BF16)
-    across(0)
-
-    t_v[...] = t_v[...] * jnp.asarray(SHRINK, BF16)
-    loads[3].wait()
-    other = 1 - z % 2
-    for i in range(2):
-        w_s[i] = u_part(other + 2 * i).astype(BF16)
-    send("w", w_s, w_r, to_z1)
-    finish(0, c)
-    for i in range(2):
-        w_v[i] = u_part(z % 2 + 2 * i)
-
-    is_z2 = grp == z2
-    is_z1 = grp == z1
-
-    @pl.when(is_z2)
-    def _():
-        x_z2.wait_recv()
-        x_z1.start()
-
     await_in("w", w_r, to_z1)
     mine, away = z // 2, 1 - z // 2
     h_s[...] = (w_v[away] + w_r[away].astype(F32)).astype(BF16)
     send("h", h_s, h_r, to_z2)
-    spread(0, c, 1)
-    spread(0, c, 2)
+    across(2)
+    spread(0, 3)
+    spread(1, 1)
+    spread(1, 2)
+    finish(2)
+
+    @pl.when(is_z2)
+    def _():
+        x_z2.wait_recv()
+        x_z1.start()
+
+    await_in("hot", oh_v.at[oc], to_y)
+    ys_v[oc] = pick(oc, c_v[oc])
+    left = ys_v.at[:, :, pl.ds(pl.multiple_of(c * half, 128), half)]
+    y_outs = [copy(("yl", i), left, yl_v, w) for i, w in enumerate([to_k, to_x, to_xk])]
+
+    @pl.when(has_span)
+    def _():
+        for out in y_outs:
+            out.start()
+        yl_v[...] = left[...]
+
+    for step in range(4):
+        relay(0, step)
+    spread(1, 3)
 
     @pl.when(jnp.logical_or(is_z1, grp == z3))
     def _():
         x_z1.wait_recv()
 
-    x_y.start()
-    sends.append(x_y)
+    send("xy", span, span, to_y)
     await_in("h", h_r, to_z2)
     u_v[c] = (w_v[mine] + w_r[mine].astype(F32) + h_r[...].astype(F32)).astype(BF16)
     send("u", u_v.at[c], u_v.at[c], to_y)
-    spread(0, c, 3)
-
-    cot_in.wait_recv()
-    product(1, oc)
-    hot_in.wait_recv()
-    ys_v[oc] = jnp.dot(oh_v[oc], c_v[oc], preferred_element_type=F32).astype(BF16)
-    left = ys_v.at[:, :, pl.ds(pl.multiple_of(c * half, 128), half)]
-    y_outs = [copy(("yl", i), left, yl_v, w) for i, w in enumerate([to_k, to_x, to_xk])]
-
-    @pl.when(has_span)
-    def _():
-        for out in y_outs:
-            out.start()
-        yl_v[...] = left[...]
-
-    across(1)
+    for step in range(1, 4):
+        spread(2, step)
     for step in range(4):
-        relay(0, c, step)
-    finish(1, oc)
-    for step in range(1, 4):
-        spread(1, oc, step)
-    collect(0, c)
-
-    outs = [pltpu.make_async_copy(
-        v_v.at[pl.ds(pl.multiple_of(c * tok, tok), tok)],
-        v_out.at[pl.ds(pl.multiple_of(c * tok, tok), tok)], out_sem.at[0])]
-    outs[0].start()
-    await_in("xl", xl_v.at[oc], to_y)
-    await_in("xy", xs_v.at[oc], to_y)
-    await_in("u", u_v.at[oc], to_y)
-    for i, (src, dst) in enumerate([(u_v, u_out), (xl_v, xl_out), (xs_v, xs_out), (ys_v, ys_out)]):
-        out = pltpu.make_async_copy(src, dst, out_sem.at[2 + i])
+        relay(1, step)
+    for step in range(4):
+        relay(2, step)
+    collect(0)
+
+    outs = []
+
+    def put(src, dst):
+        out = pltpu.make_async_copy(src, dst, out_sem.at[len(outs)])
         out.start()
         outs.append(out)
 
+    def put_v(ph):
+        block, first, count = phases[ph]
+        rows = pl.ds(pl.multiple_of(block * tok + first, count), count)
+        put(v_v.at[rows], v_out.at[rows])
+
+    put_v(0)
+    put(ys_v, ys_out)
+    collect(1)
+    put_v(1)
+    await_in("xl", xl_v.at[oc], to_y)
+    put(xl_v, xl_out)
+
     @pl.when(grp == 2 * (z // 2) + (1 - z % 2))
     def _():
         y_outs[0].wait_recv()
@@ -248,17 +269,13 @@
     def _():
         y_outs[2].wait_recv()
 
-    out = pltpu.make_async_copy(yl_v, yl_out, out_sem.at[6])
-    out.start()
-    outs.append(out)
-    for step in range(4):
-        relay(1, oc, step)
-    collect(1, oc)
-    out = pltpu.make_async_copy(
-        v_v.at[pl.ds(pl.multiple_of(oc * tok, tok), tok)],
-        v_out.at[pl.ds(pl.multiple_of(oc * tok, tok), tok)], out_sem.at[1])
-    out.start()
-    outs.append(out)
+    put(yl_v, yl_out)
+    await_in("xy", xs_v.at[oc], to_y)
+    put(xs_v, xs_out)
+    await_in("u", u_v.at[oc], to_y)
+    put(u_v, u_out)
+    collect(2)
+    put_v(2)
 
     @pl.when(has_span)
     def _():
@@ -279,7 +296,7 @@
 
 def gather(rows, tokens_in, cotangent, act_inverse, grad_inverse, n_row):
     tok, feat = tokens_in.shape
-    samples = rows.shape[0]
+    samples = rows.shape[1]
     share = grad_inverse.shape[1] // n_row
     out_rows = feat // n_row
     half = feat // 2
@@ -299,13 +316,13 @@
             vmem((2, tok, feat), BF16),
             vmem(act_inverse.shape, BF16),
             vmem((feat, share), BF16),
-            vmem((2, samples, tok), BF16),
+            vmem((2, tok, samples), BF16),
             vmem((samples, feat), BF16),
-            vmem((2, 4, piece, share), F32),
-            vmem((2, 2, piece, share), BF16),
-            vmem((2, 2, piece, share), BF16),
-            vmem((2, piece, share), BF16),
-            vmem((2, piece, share), BF16),
+            vmem((3, 4, piece, share), F32),
+            vmem((3, 2, piece, share), BF16),
+            vmem((3, 2, piece, share), BF16),
+            vmem((3, piece, share), BF16),
+            vmem((3, piece, share), BF16),
             vmem((2, tok, out_rows), BF16),
             vmem((2, tok, out_rows), BF16),
             vmem((2, tok, out_rows), F32),
@@ -313,12 +330,12 @@
             vmem((tok, out_rows), BF16),
         ] + [vmem(s, BF16) for s in shapes] + [
             pltpu.SemaphoreType.DMA((4,)),
-            pltpu.SemaphoreType.DMA((7,)),
-            pltpu.SemaphoreType.DMA((48,)),
-            pltpu.SemaphoreType.DMA((48,)),
+            pltpu.SemaphoreType.DMA((8,)),
+            pltpu.SemaphoreType.DMA((68,)),
+            pltpu.SemaphoreType.DMA((68,)),
         ],
         compiler_params=pltpu.CompilerParams(
-            collective_id=0, has_side_effects=True, vmem_limit_bytes=40 * 2 ** 20
+            collective_id=0, has_side_effects=True, vmem_limit_bytes=60 * 2 ** 20
         ),
         cost_estimate=pl.CostEstimate(flops=3 * 10 ** 9, bytes_accessed=10 ** 7, transcendentals=0),
     )(rows, tokens_in, cotangent, act_inverse, grad_inverse)
@@ -375,9 +392,8 @@
 
 
 def body_kernels(tokens_in, cotangent, sample_rows, act_inverse, grad_inverse):
-    rows = (sample_rows - lax.axis_index("col") * tokens_in.shape[0])[:, None]
     u, v, xl, xs, yl, ys = gather(
-        rows, tokens_in, cotangent, act_inverse, grad_inverse, lax.axis_size("row")
+        sample_rows[None], tokens_in, cotangent, act_inverse, grad_inverse, lax.axis_size("row")
     )
     return tuple(products(flat(u), v, flat(xl), flat(xs), flat(yl), flat(ys)))
 

time: 50.6 us -> 48.1 us (0.951)
  the two profiles are of different devices: /device:TPU:11 before, /device:TPU:0 now
where the time goes in v3:
time: 48.1 us; the launch traced here: 47.8 us
  Pallas kernels  41.2 us (86%)
  local copies, waits for them, and re-layouts  5.96 us (12%)
  between operations  0.65 us (1%)
    pallas_call x1, Pallas kernels, gather(): pl.pallas_call(gather_kernel, out_shape=[jax.ShapeDtypeStruct(s, BF16) fo...  34.9 us
    pallas_call x1, Pallas kernels, products(): pl.pallas_call(functools.partial(product_kernel, total), grid=(steps,), i...  6.25 us
    unnamed x12, local copies, waits for them, and re-layouts  5.96 us

profile of v3, /device:TPU:0, one launch (start us, length us, event | category | flops | bytes accessed | tf_op | source)
XLA Modules:
  0.0 47.8 jit_solution(6111362191300808933)
XLA Ops:
  0.6 34.9 %shard_map.76 = (bf16[2,128,384]{2,1,0:T(8,128)(2,1)}, bf16[256,3072]{1,0:T(8,128)(2,1)}, bf16[2,32,768]{2,1,0:T(8,128)(2,1)}, bf16[2,32,1536]{2,1,0:T(8,128)(2,...) custom-call(s32[1,32]{1,0:T(1,128)} %bitcast.11, bf16[128,1536]{1,0:T(8,128)(2,1)} %t_hbm.1, ...), custom_call_target="tpu_custom_call" | custom-call | flops 3000000000 | bytes 10000000 | tf_op jit(solution)/shard_map/pallas_call | solution.py:309
  35.6 0.0 copy-start
  35.6 1.4 %copy-done = bf16[256,3072]{1,0:T(8,128)(2,1)S(1)} copy-done((bf16[256,3072]{1,0:T(8,128)(2,1)S(1)}, bf16[256,3072]{1,0:T(8,128)(2,1)}, u32[]{:S(2)}) %copy-start) | copy-done | bytes 1572888
  37.0 0.0 copy-start.1
  37.0 0.9 %copy-done.1 = bf16[2,128,384]{2,1,0:T(8,128)(2,1)S(1)} copy-done((bf16[2,128,384]{2,1,0:T(8,128)(2,1)S(1)}, bf16[2,128,384]{2,1,0:T(8,128)(2,1)}, u32[]{:S(2)}) %copy-start.1) | copy-done | bytes 196632
  37.9 0.0 copy-start.2
  37.9 0.9 %copy-done.2 = bf16[2,32,1536]{2,1,0:T(8,128)(2,1)S(1)} copy-done((bf16[2,32,1536]{2,1,0:T(8,128)(2,1)S(1)}, bf16[2,32,1536]{2,1,0:T(8,128)(2,1)}, u32[]{:S(2)}) %copy-start.2) | copy-done | bytes 196632
  38.8 0.0 copy-start.3
  38.8 0.9 %copy-done.3 = bf16[2,32,1536]{2,1,0:T(8,128)(2,1)S(1)} copy-done((bf16[2,32,1536]{2,1,0:T(8,128)(2,1)S(1)}, bf16[2,32,1536]{2,1,0:T(8,128)(2,1)}, u32[]{:S(2)}) %copy-start.3) | copy-done | bytes 196632
  39.8 0.0 copy-start.4
  39.8 0.9 %copy-done.4 = bf16[2,32,768]{2,1,0:T(8,128)(2,1)S(1)} copy-done((bf16[2,32,768]{2,1,0:T(8,128)(2,1)S(1)}, bf16[2,32,768]{2,1,0:T(8,128)(2,1)}, u32[]{:S(2)}) %copy-start.4) | copy-done | bytes 98328
  40.6 0.0 copy-start.5
  40.6 0.9 %copy-done.5 = bf16[2,32,768]{2,1,0:T(8,128)(2,1)S(1)} copy-done((bf16[2,32,768]{2,1,0:T(8,128)(2,1)S(1)}, bf16[2,32,768]{2,1,0:T(8,128)(2,1)}, u32[]{:S(2)}) %copy-start.5) | copy-done | bytes 98328
  41.5 6.2 %shard_map.77 = (f32[384,3072]{1,0:T(8,128)}, f32[768,1536]{1,0:T(8,128)}, f32[768,1536]{1,0:T(8,128)}) custom-call(bf16[256,384]{1,0:T(8,128)(2,1)S(1)} %bitcast.6, bf16[256,3072]{1,0:T(8,128)(2,1)S(1)} %copy-done, bf16[64,768]{1,0:T(8,128)(2,1)S(1)} %bitcast.9, bf16[64,1536]{1,0:T(8,128)(2,1)S(1)} %bitcast.7, bf16[64,768]{1,0:T(8,128)(2,1)S(1)} %bitcast.10, ...), custom_call_target="tpu_custom_call" | custom-call | flops 1000000000 | bytes 17000000 | tf_op jit(solution)/shard_map/pallas_call | solution.py:366
Async XLA Ops:
  35.6 1.4 %copy-start = (bf16[256,3072]{1,0:T(8,128)(2,1)S(1)}, bf16[256,3072]{1,0:T(8,128)(2,1)}, u32[]{:S(2)}) copy-start(bf16[256,3072]{1,0:T(8,128)(2,1)} %get-tuple-element.10.v) | copy-start | bytes 4718596
  37.0 0.9 %copy-start.1 = (bf16[2,128,384]{2,1,0:T(8,128)(2,1)S(1)}, bf16[2,128,384]{2,1,0:T(8,128)(2,1)}, u32[]{:S(2)}) copy-start(bf16[2,128,384]{2,1,0:T(8,128)(2,1)} %get-tuple-element.9) | copy-start | bytes 589828
  37.9 0.9 %copy-start.2 = (bf16[2,32,1536]{2,1,0:T(8,128)(2,1)S(1)}, bf16[2,32,1536]{2,1,0:T(8,128)(2,1)}, u32[]{:S(2)}) copy-start(bf16[2,32,1536]{2,1,0:T(8,128)(2,1)} %get-tuple-element.12) | copy-start | bytes 589828
  38.8 0.9 %copy-start.3 = (bf16[2,32,1536]{2,1,0:T(8,128)(2,1)S(1)}, bf16[2,32,1536]{2,1,0:T(8,128)(2,1)}, u32[]{:S(2)}) copy-start(bf16[2,32,1536]{2,1,0:T(8,128)(2,1)} %get-tuple-element.14) | copy-start | bytes 589828
  39.8 0.9 %copy-start.4 = (bf16[2,32,768]{2,1,0:T(8,128)(2,1)S(1)}, bf16[2,32,768]{2,1,0:T(8,128)(2,1)}, u32[]{:S(2)}) copy-start(bf16[2,32,768]{2,1,0:T(8,128)(2,1)} %get-tuple-element.11) | copy-start | bytes 294916
  40.6 0.9 %copy-start.5 = (bf16[2,32,768]{2,1,0:T(8,128)(2,1)S(1)}, bf16[2,32,768]{2,1,0:T(8,128)(2,1)}, u32[]{:S(2)}) copy-start(bf16[2,32,768]{2,1,0:T(8,128)(2,1)} %get-tuple-element.13) | copy-start | bytes 294916

commit v4 on v3

--- a/solution.py
+++ b/solution.py
@@ -17,7 +17,7 @@
     rows_ref, t_hbm, c_hbm, a_hbm, g_hbm,
     u_out, v_out, xl_out, xs_out, yl_out, ys_out,
     t_v, c_v, a_v, g_v, oh_v, px_v, q_v, r1_s, r1_r, r2_s, r2_r,
-    w_s, w_r, w_v, h_s, h_r, u_v, v_v, xl_v, xs_v, yl_v, ys_v,
+    w_s, w_r, w_v, h_s, h_r, u_v, v_v, xl_v, xs_v, yl_v, ys_v, xlt_v, ylt_v,
     load_sem, out_sem, send_sem, recv_sem,
 ):
     grp, z, c = lax.axis_index("grp"), lax.axis_index("row"), lax.axis_index("col")
@@ -36,7 +36,7 @@
     tok = t_v.shape[0]
     share = g_v.shape[1]
     half = xl_v.shape[2]
-    out_rows = u_v.shape[2]
+    out_rows = u_v.shape[1]
     phases = ((c, 0, tok), (oc, 0, tok // 2), (oc, tok // 2, tok // 2))
 
     names = {}
@@ -57,13 +57,23 @@
     def await_in(name, dst, where):
         copy(name, dst, dst, where).wait_recv()
 
+    def load_a(block, sem):
+        rows = pl.ds(pl.multiple_of(block * out_rows, out_rows), out_rows)
+        return pltpu.make_async_copy(a_hbm.at[rows], a_v.at[rows], load_sem.at[sem])
+
+    odd = z % 2
+    away_blocks = (1 - odd, 3 - odd)
+    home_blocks = (odd, 2 + odd)
     loads = [
+        pltpu.make_async_copy(t_hbm, t_v, load_sem.at[2]),
+        load_a(away_blocks[0], 3),
+        load_a(away_blocks[1], 4),
         pltpu.make_async_copy(c_hbm, c_v.at[c], load_sem.at[0]),
         pltpu.make_async_copy(
             g_hbm.at[:, pl.ds(pl.multiple_of(z * share, 128), share)], g_v, load_sem.at[1]
         ),
-        pltpu.make_async_copy(t_hbm, t_v, load_sem.at[2]),
-        pltpu.make_async_copy(a_hbm, a_v, load_sem.at[3]),
+        load_a(home_blocks[0], 5),
+        load_a(home_blocks[1], 6),
     ]
     for load in loads:
         load.start()
@@ -160,18 +170,7 @@
     x_z1 = copy("x1", span, span, to_z1)
 
     loads[0].wait()
-    loads[1].wait()
-    product(0)
-    loads[2].wait()
     px_v[...] = pick(c, t_v[...])
-    t_v[...] = t_v[...] * jnp.asarray(SHRINK, BF16)
-    ys_v[c] = pick(c, c_v[c])
-    across(0)
-
-    loads[3].wait()
-    for i in range(2):
-        w_s[i] = u_part(1 - z % 2 + 2 * i).astype(BF16)
-    send("w", w_s, w_r, to_z1)
 
     @pl.when(has_span)
     def _():
@@ -179,61 +178,89 @@
         x_z2.start()
         x_z1.start()
 
+    t_v[...] = t_v[...] * jnp.asarray(SHRINK, BF16)
+    for i in range(2):
+        loads[1 + i].wait()
+        w_s[i] = u_part(away_blocks[i]).astype(BF16)
+    send("w", w_s, w_r, to_z1)
+    loads[3].wait()
+    loads[4].wait()
+    product(0)
+    ys_v[c] = pick(c, c_v[c])
+
+    def y_copies(block):
+        left = ys_v.at[block, :, pl.ds(pl.multiple_of(c * half, 128), half)]
+        own = 0 if block is c else 1
+        return left, [
+            copy(("yl", own, i), left, yl_v.at[block], w) for i, w in enumerate([to_k, to_x, to_xk])
+        ]
+
+    left_c, y_c = y_copies(c)
+    left_oc, y_oc = y_copies(oc)
+
+    @pl.when(has_span)
+    def _():
+        for out in y_c:
+            out.start()
+        yl_v[c] = left_c[...]
+
+    across(0)
+    for i in range(2):
+        loads[5 + i].wait()
+        w_v[i] = u_part(home_blocks[i])
     finish(0)
     await_cot(1)
     product(1)
-    for i in range(2):
-        w_v[i] = u_part(z % 2 + 2 * i)
+
+    @pl.when(is_z2)
+    def _():
+        x_z2.wait_recv()
+        x_z1.start()
+
     across(1)
-    finish(1)
-    spread(0, 1)
-    spread(0, 2)
-    await_cot(2)
-    product(2)
-    send("xl", at_half(px_v, oc), xl_v.at[c], to_y)
-    xl_v[c] = at_half(px_v, c)[...]
     await_in("w", w_r, to_z1)
     mine, away = z // 2, 1 - z // 2
     h_s[...] = (w_v[away] + w_r[away].astype(F32)).astype(BF16)
     send("h", h_s, h_r, to_z2)
+    spread(0, 1)
+    finish(1)
+    spread(0, 2)
+    await_cot(2)
+    product(2)
+    spread(0, 3)
     across(2)
-    spread(0, 3)
+    send("xl", at_half(px_v, oc), xl_v.at[c], to_y)
+    xl_v[c] = at_half(px_v, c)[...]
     spread(1, 1)
     spread(1, 2)
+
+    @pl.when(jnp.logical_or(is_z1, grp == z3))
+    def _():
+        x_z1.wait_recv()
+
+    send("xy", span, span, to_y)
     finish(2)
-
-    @pl.when(is_z2)
-    def _():
-        x_z2.wait_recv()
-        x_z1.start()
-
     await_in("hot", oh_v.at[oc], to_y)
     ys_v[oc] = pick(oc, c_v[oc])
-    left = ys_v.at[:, :, pl.ds(pl.multiple_of(c * half, 128), half)]
-    y_outs = [copy(("yl", i), left, yl_v, w) for i, w in enumerate([to_k, to_x, to_xk])]
 
     @pl.when(has_span)
     def _():
-        for out in y_outs:
+        for out in y_oc:
             out.start()
-        yl_v[...] = left[...]
+        yl_v[oc] = left_oc[...]
 
     for step in range(4):
         relay(0, step)
     spread(1, 3)
-
-    @pl.when(jnp.logical_or(is_z1, grp == z3))
-    def _():
-        x_z1.wait_recv()
-
-    send("xy", span, span, to_y)
     await_in("h", h_r, to_z2)
-    u_v[c] = (w_v[mine] + w_r[mine].astype(F32) + h_r[...].astype(F32)).astype(BF16)
+    u = w_v[mine] + w_r[mine].astype(F32) + h_r[...].astype(F32)
+    u_v[c] = u.T.astype(BF16)
     send("u", u_v.at[c], u_v.at[c], to_y)
+    for step in range(3):
+        relay(1, step)
     for step in range(1, 4):
         spread(2, step)
-    for step in range(4):
-        relay(1, step)
+    relay(1, 3)
     for step in range(4):
         relay(2, step)
     collect(0)
@@ -255,25 +282,31 @@
     collect(1)
     put_v(1)
     await_in("xl", xl_v.at[oc], to_y)
-    put(xl_v, xl_out)
+    xlt_v[...] = xl_v[...].reshape(xlt_v.shape[::-1]).T
+    put(xlt_v, xl_out)
 
     @pl.when(grp == 2 * (z // 2) + (1 - z % 2))
     def _():
-        y_outs[0].wait_recv()
+        y_c[0].wait_recv()
+        y_oc[0].wait_recv()
 
     @pl.when(grp == 2 * (1 - z // 2) + z % 2)
     def _():
-        y_outs[1].wait_recv()
+        y_c[1].wait_recv()
+        y_oc[1].wait_recv()
 
     @pl.when(grp == 2 * (1 - z // 2) + (1 - z % 2))
     def _():
-        y_outs[2].wait_recv()
-
-    put(yl_v, yl_out)
+        y_c[2].wait_recv()
+        y_oc[2].wait_recv()
+
+    ylt_v[...] = yl_v[...].reshape(ylt_v.shape[::-1]).T
+    put(ylt_v, yl_out)
     await_in("xy", xs_v.at[oc], to_y)
     put(xs_v, xs_out)
     await_in("u", u_v.at[oc], to_y)
-    put(u_v, u_out)
+    for block in range(2):
+        put(u_v.at[block], u_out.at[:, block * tok:(block + 1) * tok])
     collect(2)
     put_v(2)
 
@@ -281,7 +314,7 @@
     def _():
         x_z2.wait_send()
         x_z1.wait_send()
-        for out in y_outs:
+        for out in y_c + y_oc:
             out.wait_send()
 
     @pl.when(is_z2)
@@ -301,10 +334,10 @@
     out_rows = feat // n_row
     half = feat // 2
     piece = tok // 4
-    shapes = [
-        (2, tok, out_rows), (2 * tok, grad_inverse.shape[1]),
-        (2, samples, half), (2, samples, feat), (2, samples, half), (2, samples, feat),
-    ]
+    v_shape, span = (2 * tok, grad_inverse.shape[1]), (2, samples, feat)
+    left, left_t = (2, samples, half), (half, 2 * samples)
+    shapes = [(out_rows, 2 * tok), v_shape, left_t, span, left_t, span]
+    held = [(2, out_rows, tok), v_shape, left, span, left, span, left_t, left_t]
     vmem = pltpu.VMEM
     return pl.pallas_call(
         gather_kernel,
@@ -328,11 +361,11 @@
             vmem((2, tok, out_rows), F32),
             vmem((tok, out_rows), BF16),
             vmem((tok, out_rows), BF16),
-        ] + [vmem(s, BF16) for s in shapes] + [
-            pltpu.SemaphoreType.DMA((4,)),
-            pltpu.SemaphoreType.DMA((8,)),
-            pltpu.SemaphoreType.DMA((68,)),
-            pltpu.SemaphoreType.DMA((68,)),
+        ] + [vmem(s, BF16) for s in held] + [
+            pltpu.SemaphoreType.DMA((7,)),
+            pltpu.SemaphoreType.DMA((9,)),
+            pltpu.SemaphoreType.DMA((72,)),
+            pltpu.SemaphoreType.DMA((72,)),
         ],
         compiler_params=pltpu.CompilerParams(
             collective_id=0, has_side_effects=True, vmem_limit_bytes=60 * 2 ** 20
@@ -341,21 +374,15 @@
     )(rows, tokens_in, cotangent, act_inverse, grad_inverse)
 
 
-def product_kernel(total, u, v, xl, xs, yl, ys, p_out, a_out, g_out, ut, xt, yt):
-    @pl.when(pl.program_id(0) == 0)
-    def _():
-        ut[...] = u[...].T
-        xt[...] = xl[...].T
-        yt[...] = yl[...].T
-
+def product_kernel(total, ut, v, xt, xs, yt, ys, p_out, a_out, g_out):
     a_out[...] = jnp.dot(xt[...], xs[...], preferred_element_type=F32) * (1 / total)
     g_out[...] = jnp.dot(yt[...], ys[...], preferred_element_type=F32) * (1 / total)
     p_out[...] = jnp.dot(ut[...], v[...], preferred_element_type=F32) * (1 / SHRINK)
 
 
-def products(u, v, xl, xs, yl, ys):
+def products(ut, v, xt, xs, yt, ys):
     steps = 6
-    total = xl.shape[0]
+    total = xt.shape[1]
 
     def whole(a):
         return pl.BlockSpec(a.shape, lambda i: (0, 0))
@@ -367,24 +394,20 @@
         functools.partial(product_kernel, total),
         grid=(steps,),
         in_specs=[
-            whole(u), cut(v.shape[0], v.shape[1]),
-            whole(xl), cut(total, xs.shape[1]), whole(yl), cut(total, ys.shape[1]),
+            whole(ut), cut(v.shape[0], v.shape[1]),
+            whole(xt), cut(total, xs.shape[1]), whole(yt), cut(total, ys.shape[1]),
         ],
         out_specs=[
-            cut(u.shape[1], v.shape[1]), cut(xl.shape[1], xs.shape[1]), cut(yl.shape[1], ys.shape[1])
+            cut(ut.shape[0], v.shape[1]), cut(xt.shape[0], xs.shape[1]), cut(yt.shape[0], ys.shape[1])
         ],
         out_shape=[
-            jax.ShapeDtypeStruct((u.shape[1], v.shape[1]), F32),
-            jax.ShapeDtypeStruct((xl.shape[1], xs.shape[1]), F32),
-            jax.ShapeDtypeStruct((yl.shape[1], ys.shape[1]), F32),
+            jax.ShapeDtypeStruct((ut.shape[0], v.shape[1]), F32),
+            jax.ShapeDtypeStruct((xt.shape[0], xs.shape[1]), F32),
+            jax.ShapeDtypeStruct((yt.shape[0], ys.shape[1]), F32),
         ],
-        scratch_shapes=[
-            pltpu.VMEM(u.shape[::-1], BF16), pltpu.VMEM(xl.shape[::-1], BF16),
-            pltpu.VMEM(yl.shape[::-1], BF16),
-        ],
-        compiler_params=pltpu.CompilerParams(vmem_limit_bytes=40 * 2 ** 20),
+        compiler_params=pltpu.CompilerParams(vmem_limit_bytes=60 * 2 ** 20),
         cost_estimate=pl.CostEstimate(flops=10 ** 9, bytes_accessed=17 * 10 ** 6, transcendentals=0),
-    )(u, v, xl, xs, yl, ys)
+    )(ut, v, xt, xs, yt, ys)
 
 
 def flat(a):
@@ -392,10 +415,10 @@
 
 
 def body_kernels(tokens_in, cotangent, sample_rows, act_inverse, grad_inverse):
-    u, v, xl, xs, yl, ys = gather(
+    ut, v, xt, xs, yt, ys = gather(
         sample_rows[None], tokens_in, cotangent, act_inverse, grad_inverse, lax.axis_size("row")
     )
-    return tuple(products(flat(u), v, flat(xl), flat(xs), flat(yl), flat(ys)))
+    return tuple(products(ut, v, xt, flat(xs), yt, flat(ys)))
 
 
 def body(tokens_in, cotangent, sample_rows, act_inverse, grad_inverse):

time: 48.1 us -> 43.6 us (0.906)
  local copies, waits for them, and re-layouts: 5.96 us -> 0 us
  Pallas kernels: 41.2 us -> 42.7 us
    unnamed x12 -> x0, local copies, waits for them, and re-layouts: 5.96 us -> none
    pallas_call x1, Pallas kernels: 6.25 us -> 7.62 us  [products(): pl.pallas_call(functools.partial(product_kernel, total), grid=(steps,), i...]
where the time goes in v4:
time: 43.6 us; the launch traced here: 43.3 us
  Pallas kernels  42.7 us (98%)
  between operations  0.64 us (1%)
    pallas_call x1, Pallas kernels, gather(): pl.pallas_call(gather_kernel, out_shape=[jax.ShapeDtypeStruct(s, BF16) fo...  35.1 us
    pallas_call x1, Pallas kernels, products(): pl.pallas_call(functools.partial(product_kernel, total), grid=(steps,), i...  7.62 us

profile of v4, /device:TPU:0, one launch (start us, length us, event | category | flops | bytes accessed | tf_op | source)
XLA Modules:
  0.0 43.3 jit_solution(13408286560879861567)
XLA Ops:
  0.6 35.1 %shard_map.76 = (bf16[384,256]{1,0:T(8,128)(2,1)}, bf16[256,3072]{1,0:T(8,128)(2,1)}, bf16[768,64]{1,0:T(8,128)(2,1)}, bf16[2,32,1536]{2,1,0:T(8,128)(2,1)}, bf1...) custom-call(s32[1,32]{1,0:T(1,128)} %bitcast.3, bf16[128,1536]{1,0:T(8,128)(2,1)} %t_hbm.1, bf16[128,1536]{1,0:T(8,128)(2,1)} %c_hbm.1, ...), custom_call_target="tpu_custom_call" | custom-call | flops 3000000000 | bytes 10000000 | tf_op jit(solution)/shard_map/pallas_call | solution.py:342
  35.7 7.6 %shard_map.77 = (f32[384,3072]{1,0:T(8,128)}, f32[768,1536]{1,0:T(8,128)}, f32[768,1536]{1,0:T(8,128)}) custom-call(bf16[384,256]{1,0:T(8,128)(2,1)} %get-tuple-element.9.ut, bf16[256,3072]{1,0:T(8,128)(2,1)} %get-tuple-element.10.v, bf16[768,64]{1,0:T(8,128)(2,1)} %get-tuple-element.11.xt, bf16[64,1536]{1,0:T(8,128)(2,1)} %bitcast.4, ...), custom_call_target="tpu_custom_call" | custom-call | flops 1000000000 | bytes 17000000 | tf_op jit(solution)/shard_map/pallas_call | solution.py:393

commit v5 on v4

--- a/solution.py
+++ b/solution.py
@@ -17,6 +17,7 @@
     rows_ref, t_hbm, c_hbm, a_hbm, g_hbm,
     u_out, v_out, xl_out, xs_out, yl_out, ys_out,
     t_v, c_v, a_v, g_v, oh_v, px_v, q_v, r1_s, r1_r, r2_s, r2_r,
+    qb_v, b1_s, b1_r, b2_s, b2_r,
     w_s, w_r, w_v, h_s, h_r, u_v, v_v, xl_v, xs_v, yl_v, ys_v, xlt_v, ylt_v,
     load_sem, out_sem, send_sem, recv_sem,
 ):
@@ -34,7 +35,7 @@
     to_z1 = {"row": z1}
     to_z2 = {"row": z2}
     tok = t_v.shape[0]
-    share = g_v.shape[1]
+    share = g_v.shape[2]
     half = xl_v.shape[2]
     out_rows = u_v.shape[1]
     phases = ((c, 0, tok), (oc, 0, tok // 2), (oc, tok // 2, tok // 2))
@@ -60,6 +61,10 @@
     def load_a(block, sem):
         rows = pl.ds(pl.multiple_of(block * out_rows, out_rows), out_rows)
         return pltpu.make_async_copy(a_hbm.at[rows], a_v.at[rows], load_sem.at[sem])
+
+    def load_g(part, sem):
+        columns = pl.ds(pl.multiple_of(part * share, 128), share)
+        return pltpu.make_async_copy(g_hbm.at[:, columns], g_v.at[part], load_sem.at[sem])
 
     odd = z % 2
     away_blocks = (1 - odd, 3 - odd)
@@ -69,12 +74,10 @@
         load_a(away_blocks[0], 3),
         load_a(away_blocks[1], 4),
         pltpu.make_async_copy(c_hbm, c_v.at[c], load_sem.at[0]),
-        pltpu.make_async_copy(
-            g_hbm.at[:, pl.ds(pl.multiple_of(z * share, 128), share)], g_v, load_sem.at[1]
-        ),
+        load_g(z, 1),
         load_a(home_blocks[0], 5),
         load_a(home_blocks[1], 6),
-    ]
+    ] + [load_g((z + i) % 4, 6 + i) for i in range(1, 4)]
     for load in loads:
         load.start()
 
@@ -107,7 +110,7 @@
 
     def product(ph):
         block, first, count = phases[ph]
-        q = jnp.dot(c_v[block, first:first + count], g_v[...], preferred_element_type=F32)
+        q = jnp.dot(c_v[block, first:first + count], g_v[z], preferred_element_type=F32)
         q_v[ph, :, cut(ph)] = q.reshape(4, count // 4, share)
         r1_s[ph, :, cut(ph)] = q_v[ph, pl.ds(2 * ok, 2), cut(ph)].astype(BF16)
         send(("r1", ph), r1_s.at[ph, :, cut(ph)], r1_r.at[ph, :, cut(ph)], to_k)
@@ -151,6 +154,45 @@
         for step in range(4):
             await_in(("vk", ph, 4 + step), v_at(ph, ok, ox, step), to_k)
 
+    def rows_b(ph, core):
+        block, first, count = phases[ph]
+        return pl.ds(pl.multiple_of(block * tok + first + core * (count // 2), count // 2), count // 2)
+
+    def product_b(ph, j):
+        block, first, count = phases[ph]
+        unit = 4 * (ph - 1) + j
+        q = jnp.dot(c_v[block, first:first + count], g_v[j], preferred_element_type=F32)
+        qb_v[unit] = q.reshape(2, count // 2, share)
+        b1_s[unit] = qb_v[unit, ok].astype(BF16)
+        send(("b1", unit), b1_s.at[unit], b1_r.at[unit], to_k)
+
+    def across_b(ph, j):
+        unit = 4 * (ph - 1) + j
+        await_in(("b1", unit), b1_r.at[unit], to_k)
+        total = qb_v[unit, k] + b1_r[unit].astype(F32)
+        qb_v[unit, k] = total
+        b2_s[unit] = total.astype(BF16)
+        send(("b2", unit), b2_s.at[unit], b2_r.at[unit], to_x)
+
+    def finish_b(ph, j):
+        unit = 4 * (ph - 1) + j
+        await_in(("b2", unit), b2_r.at[unit], to_x)
+        mine = v_v.at[rows_b(ph, k), j * share:(j + 1) * share]
+        mine[...] = (qb_v[unit, k] + b2_r[unit].astype(F32)).astype(BF16)
+        send(("bk", unit), mine, mine, to_k)
+
+    def collect_b(ph):
+        for j in range(4):
+            got = v_v.at[rows_b(ph, ok), j * share:(j + 1) * share]
+            await_in(("bk", 4 * (ph - 1) + j), got, to_k)
+
+    def run_b(ph):
+        product_b(ph, 0)
+        for j in range(1, 4):
+            product_b(ph, j)
+            across_b(ph, j - 1)
+        across_b(ph, 3)
+
     def u_part(block):
         rows = a_v[pl.ds(pl.multiple_of(block * out_rows, out_rows), out_rows), :]
         return lax.dot_general(t_v[...], rows, (((1,), (1,)), ((), ())), preferred_element_type=F32)
@@ -210,36 +252,34 @@
         w_v[i] = u_part(home_blocks[i])
     finish(0)
     await_cot(1)
-    product(1)
+    for i in range(7, 10):
+        loads[i].wait()
+    run_b(1)
 
     @pl.when(is_z2)
     def _():
         x_z2.wait_recv()
         x_z1.start()
 
-    across(1)
     await_in("w", w_r, to_z1)
     mine, away = z // 2, 1 - z // 2
     h_s[...] = (w_v[away] + w_r[away].astype(F32)).astype(BF16)
     send("h", h_s, h_r, to_z2)
     spread(0, 1)
-    finish(1)
     spread(0, 2)
     await_cot(2)
-    product(2)
+    run_b(2)
     spread(0, 3)
-    across(2)
+    for j in range(4):
+        finish_b(1, j)
     send("xl", at_half(px_v, oc), xl_v.at[c], to_y)
     xl_v[c] = at_half(px_v, c)[...]
-    spread(1, 1)
-    spread(1, 2)
 
     @pl.when(jnp.logical_or(is_z1, grp == z3))
     def _():
         x_z1.wait_recv()
 
     send("xy", span, span, to_y)
-    finish(2)
     await_in("hot", oh_v.at[oc], to_y)
     ys_v[oc] = pick(oc, c_v[oc])
 
@@ -249,20 +289,14 @@
             out.start()
         yl_v[oc] = left_oc[...]
 
-    for step in range(4):
-        relay(0, step)
-    spread(1, 3)
     await_in("h", h_r, to_z2)
     u = w_v[mine] + w_r[mine].astype(F32) + h_r[...].astype(F32)
     u_v[c] = u.T.astype(BF16)
     send("u", u_v.at[c], u_v.at[c], to_y)
-    for step in range(3):
-        relay(1, step)
-    for step in range(1, 4):
-        spread(2, step)
-    relay(1, 3)
     for step in range(4):
-        relay(2, step)
+        relay(0, step)
+    for j in range(4):
+        finish_b(2, j)
     collect(0)
 
     outs = []
@@ -279,7 +313,7 @@
 
     put_v(0)
     put(ys_v, ys_out)
-    collect(1)
+    collect_b(1)
     put_v(1)
     await_in("xl", xl_v.at[oc], to_y)
     xlt_v[...] = xl_v[...].reshape(xlt_v.shape[::-1]).T
@@ -307,7 +341,7 @@
     await_in("u", u_v.at[oc], to_y)
     for block in range(2):
         put(u_v.at[block], u_out.at[:, block * tok:(block + 1) * tok])
-    collect(2)
+    collect_b(2)
     put_v(2)
 
     @pl.when(has_span)
@@ -348,21 +382,26 @@
             vmem((tok, feat), BF16),
             vmem((2, tok, feat), BF16),
             vmem(act_inverse.shape, BF16),
-            vmem((feat, share), BF16),
+            vmem((n_row, feat, share), BF16),
             vmem((2, tok, samples), BF16),
             vmem((samples, feat), BF16),
-            vmem((3, 4, piece, share), F32),
-            vmem((3, 2, piece, share), BF16),
-            vmem((3, 2, piece, share), BF16),
-            vmem((3, piece, share), BF16),
-            vmem((3, piece, share), BF16),
+            vmem((1, 4, piece, share), F32),
+            vmem((1, 2, piece, share), BF16),
+            vmem((1, 2, piece, share), BF16),
+            vmem((1, piece, share), BF16),
+            vmem((1, piece, share), BF16),
+            vmem((8, 2, piece, share), F32),
+            vmem((8, piece, share), BF16),
+            vmem((8, piece, share), BF16),
+            vmem((8, piece, share), BF16),
+            vmem((8, piece, share), BF16),
             vmem((2, tok, out_rows), BF16),
             vmem((2, tok, out_rows), BF16),
             vmem((2, tok, out_rows), F32),
             vmem((tok, out_rows), BF16),
             vmem((tok, out_rows), BF16),
         ] + [vmem(s, BF16) for s in held] + [
-            pltpu.SemaphoreType.DMA((7,)),
+            pltpu.SemaphoreType.DMA((10,)),
             pltpu.SemaphoreType.DMA((9,)),
             pltpu.SemaphoreType.DMA((72,)),
             pltpu.SemaphoreType.DMA((72,)),

time: 43.6 us -> 40.2 us (0.922)
  Pallas kernels: 42.7 us -> 39.3 us
    pallas_call x1, Pallas kernels: 35.1 us -> 31.7 us  [gather(): pl.pallas_call(gather_kernel, out_shape=[jax.ShapeDtypeStruct(s, BF16) fo...]
where the time goes in v5:
time: 40.2 us; the launch traced here: 39.9 us
  Pallas kernels  39.3 us (98%)
  between operations  0.64 us (2%)
    pallas_call x1, Pallas kernels, gather(): pl.pallas_call(gather_kernel, out_shape=[jax.ShapeDtypeStruct(s, BF16) fo...  31.7 us
    pallas_call x1, Pallas kernels, products(): pl.pallas_call(functools.partial(product_kernel, total), grid=(steps,), i...  7.62 us

profile of v5, /device:TPU:0, one launch (start us, length us, event | category | flops | bytes accessed | tf_op | source)
XLA Modules:
  0.0 39.9 jit_solution(4666853710618990179)
XLA Ops:
  0.6 31.7 %shard_map.76 = (bf16[384,256]{1,0:T(8,128)(2,1)}, bf16[256,3072]{1,0:T(8,128)(2,1)}, bf16[768,64]{1,0:T(8,128)(2,1)}, bf16[2,32,1536]{2,1,0:T(8,128)(2,1)}, bf1...) custom-call(s32[1,32]{1,0:T(1,128)} %bitcast.3, bf16[128,1536]{1,0:T(8,128)(2,1)} %t_hbm.1, bf16[128,1536]{1,0:T(8,128)(2,1)} %c_hbm.1, ...), custom_call_target="tpu_custom_call" | custom-call | flops 3000000000 | bytes 10000000 | tf_op jit(solution)/shard_map/pallas_call | solution.py:376
  32.3 7.6 %shard_map.77 = (f32[384,3072]{1,0:T(8,128)}, f32[768,1536]{1,0:T(8,128)}, f32[768,1536]{1,0:T(8,128)}) custom-call(bf16[384,256]{1,0:T(8,128)(2,1)} %get-tuple-element.9.ut, bf16[256,3072]{1,0:T(8,128)(2,1)} %get-tuple-element.10.v, bf16[768,64]{1,0:T(8,128)(2,1)} %get-tuple-element.11.xt, bf16[64,1536]{1,0:T(8,128)(2,1)} %bitcast.4, ...), custom_call_target="tpu_custom_call" | custom-call | flops 1000000000 | bytes 17000000 | tf_op jit(solution)/shard_map/pallas_call | solution.py:432

commit v6 on v4

--- a/solution.py
+++ b/solution.py
@@ -17,6 +17,7 @@
     rows_ref, t_hbm, c_hbm, a_hbm, g_hbm,
     u_out, v_out, xl_out, xs_out, yl_out, ys_out,
     t_v, c_v, a_v, g_v, oh_v, px_v, q_v, r1_s, r1_r, r2_s, r2_r,
+    qb_v, b1_s, b1_r, b2_s, b2_r,
     w_s, w_r, w_v, h_s, h_r, u_v, v_v, xl_v, xs_v, yl_v, ys_v, xlt_v, ylt_v,
     load_sem, out_sem, send_sem, recv_sem,
 ):
@@ -34,7 +35,7 @@
     to_z1 = {"row": z1}
     to_z2 = {"row": z2}
     tok = t_v.shape[0]
-    share = g_v.shape[1]
+    share = g_v.shape[2]
     half = xl_v.shape[2]
     out_rows = u_v.shape[1]
     phases = ((c, 0, tok), (oc, 0, tok // 2), (oc, tok // 2, tok // 2))
@@ -60,6 +61,10 @@
     def load_a(block, sem):
         rows = pl.ds(pl.multiple_of(block * out_rows, out_rows), out_rows)
         return pltpu.make_async_copy(a_hbm.at[rows], a_v.at[rows], load_sem.at[sem])
+
+    def load_g(part, sem):
+        columns = pl.ds(pl.multiple_of(part * share, 128), share)
+        return pltpu.make_async_copy(g_hbm.at[:, columns], g_v.at[part], load_sem.at[sem])
 
     odd = z % 2
     away_blocks = (1 - odd, 3 - odd)
@@ -69,12 +74,10 @@
         load_a(away_blocks[0], 3),
         load_a(away_blocks[1], 4),
         pltpu.make_async_copy(c_hbm, c_v.at[c], load_sem.at[0]),
-        pltpu.make_async_copy(
-            g_hbm.at[:, pl.ds(pl.multiple_of(z * share, 128), share)], g_v, load_sem.at[1]
-        ),
+        load_g(z, 1),
         load_a(home_blocks[0], 5),
         load_a(home_blocks[1], 6),
-    ]
+    ] + [load_g((z + i) % 4, 6 + i) for i in range(1, 4)]
     for load in loads:
         load.start()
 
@@ -84,9 +87,20 @@
         pl.semaphore_signal(barrier, inc=1, device_id=where, device_id_type=pl.DeviceIdType.MESH)
     pl.semaphore_wait(barrier, len(partners))
 
-    for ph in (1, 2):
-        part = pl.ds(phases[ph][1], phases[ph][2])
-        send(("cot", ph), c_hbm.at[part], c_v.at[c, part], to_y)
+    feat = t_v.shape[1]
+    chunks = (
+        (pl.ds(0, tok // 2), pl.ds(0, feat)),
+        (pl.ds(tok // 2, tok // 2), pl.ds(0, feat // 2)),
+        (pl.ds(tok // 2, tok // 2), pl.ds(feat // 2, feat // 2)),
+    )
+
+    def send_cot(i):
+        send(("cot", i), c_hbm.at[chunks[i]], c_v.at[(c,) + chunks[i]], to_y)
+
+    def await_cot(i):
+        await_in(("cot", i), c_v.at[(oc,) + chunks[i]], to_y)
+
+    send_cot(0)
 
     hot = lax.broadcasted_iota(jnp.int32, (tok, rows_ref.shape[1]), 0) + c * tok == rows_ref[...]
     oh_v[c] = jnp.where(hot, 1.0, 0.0).astype(BF16)
@@ -107,7 +121,7 @@
 
     def product(ph):
         block, first, count = phases[ph]
-        q = jnp.dot(c_v[block, first:first + count], g_v[...], preferred_element_type=F32)
+        q = jnp.dot(c_v[block, first:first + count], g_v[z], preferred_element_type=F32)
         q_v[ph, :, cut(ph)] = q.reshape(4, count // 4, share)
         r1_s[ph, :, cut(ph)] = q_v[ph, pl.ds(2 * ok, 2), cut(ph)].astype(BF16)
         send(("r1", ph), r1_s.at[ph, :, cut(ph)], r1_r.at[ph, :, cut(ph)], to_k)
@@ -151,16 +165,45 @@
         for step in range(4):
             await_in(("vk", ph, 4 + step), v_at(ph, ok, ox, step), to_k)
 
+    def rows_b(core):
+        block, first, count = phases[2]
+        return pl.ds(pl.multiple_of(block * tok + first + core * (count // 2), count // 2), count // 2)
+
+    def half_b(j, side):
+        mid = feat // 2
+        block = c_v[oc, tok // 2:, side * mid:(side + 1) * mid]
+        part = g_v[j, side * mid:(side + 1) * mid]
+        return jnp.dot(block, part, preferred_element_type=F32).reshape(2, tok // 4, share)
+
+    def product_b(j):
+        qb_v[j] = qb_v[j] + half_b(j, 1)
+        b1_s[j] = qb_v[j, ok].astype(BF16)
+        send(("b1", j), b1_s.at[j], b1_r.at[j], to_k)
+
+    def across_b(j):
+        await_in(("b1", j), b1_r.at[j], to_k)
+        total = qb_v[j, k] + b1_r[j].astype(F32)
+        qb_v[j, k] = total
+        b2_s[j] = total.astype(BF16)
+        send(("b2", j), b2_s.at[j], b2_r.at[j], to_x)
+
+    def finish_b(j):
+        await_in(("b2", j), b2_r.at[j], to_x)
+        mine = v_v.at[rows_b(k), j * share:(j + 1) * share]
+        mine[...] = (qb_v[j, k] + b2_r[j].astype(F32)).astype(BF16)
+        send(("bk", j), mine, mine, to_k)
+
+    def collect_b():
+        for j in range(4):
+            got = v_v.at[rows_b(ok), j * share:(j + 1) * share]
+            await_in(("bk", j), got, to_k)
+
     def u_part(block):
         rows = a_v[pl.ds(pl.multiple_of(block * out_rows, out_rows), out_rows), :]
         return lax.dot_general(t_v[...], rows, (((1,), (1,)), ((), ())), preferred_element_type=F32)
 
     def at_half(ref, index):
         return ref.at[:, pl.ds(pl.multiple_of(index * half, 128), half)]
-
-    def await_cot(ph):
-        part = pl.ds(phases[ph][1], phases[ph][2])
-        await_in(("cot", ph), c_v.at[oc, part], to_y)
 
     has_span = grp == z
     is_z2 = grp == z2
@@ -183,9 +226,11 @@
         loads[1 + i].wait()
         w_s[i] = u_part(away_blocks[i]).astype(BF16)
     send("w", w_s, w_r, to_z1)
+    send_cot(1)
     loads[3].wait()
     loads[4].wait()
     product(0)
+    send_cot(2)
     ys_v[c] = pick(c, c_v[c])
 
     def y_copies(block):
@@ -209,7 +254,7 @@
         loads[5 + i].wait()
         w_v[i] = u_part(home_blocks[i])
     finish(0)
-    await_cot(1)
+    await_cot(0)
     product(1)
 
     @pl.when(is_z2)
@@ -225,44 +270,48 @@
     spread(0, 1)
     finish(1)
     spread(0, 2)
+    for i in range(7, 10):
+        loads[i].wait()
+    await_cot(1)
+    for j in range(4):
+        qb_v[j] = half_b(j, 0)
+    spread(0, 3)
     await_cot(2)
-    product(2)
-    spread(0, 3)
-    across(2)
+    product_b(0)
+    product_b(1)
+    product_b(2)
+    across_b(0)
+    product_b(3)
+    for j in range(1, 4):
+        across_b(j)
+    for step in range(1, 4):
+        spread(1, step)
     send("xl", at_half(px_v, oc), xl_v.at[c], to_y)
     xl_v[c] = at_half(px_v, c)[...]
-    spread(1, 1)
-    spread(1, 2)
 
     @pl.when(jnp.logical_or(is_z1, grp == z3))
     def _():
         x_z1.wait_recv()
 
     send("xy", span, span, to_y)
-    finish(2)
-    await_in("hot", oh_v.at[oc], to_y)
-    ys_v[oc] = pick(oc, c_v[oc])
-
-    @pl.when(has_span)
-    def _():
-        for out in y_oc:
-            out.start()
-        yl_v[oc] = left_oc[...]
-
-    for step in range(4):
-        relay(0, step)
-    spread(1, 3)
     await_in("h", h_r, to_z2)
     u = w_v[mine] + w_r[mine].astype(F32) + h_r[...].astype(F32)
     u_v[c] = u.T.astype(BF16)
     send("u", u_v.at[c], u_v.at[c], to_y)
-    for step in range(3):
-        relay(1, step)
-    for step in range(1, 4):
-        spread(2, step)
-    relay(1, 3)
-    for step in range(4):
-        relay(2, step)
+    await_in("hot", oh_v.at[oc], to_y)
+    ys_v[oc] = pick(oc, c_v[oc])
+
+    @pl.when(has_span)
+    def _():
+        for out in y_oc:
+            out.start()
+        yl_v[oc] = left_oc[...]
+
+    for ph in range(2):
+        for step in range(4):
+            relay(ph, step)
+    for j in range(4):
+        finish_b(j)
     collect(0)
 
     outs = []
@@ -307,7 +356,7 @@
     await_in("u", u_v.at[oc], to_y)
     for block in range(2):
         put(u_v.at[block], u_out.at[:, block * tok:(block + 1) * tok])
-    collect(2)
+    collect_b()
     put_v(2)
 
     @pl.when(has_span)
@@ -341,34 +390,39 @@
     vmem = pltpu.VMEM
     return pl.pallas_call(
         gather_kernel,
-        out_shape=[jax.ShapeDtypeStruct(s, BF16) for s in shapes],
+        out_shape=[vmem(s, BF16) for s in shapes],
         in_specs=[pl.BlockSpec(memory_space=vmem)] + [pl.BlockSpec(memory_space=pl.ANY)] * 4,
         out_specs=[pl.BlockSpec(memory_space=pl.ANY)] * 6,
         scratch_shapes=[
             vmem((tok, feat), BF16),
             vmem((2, tok, feat), BF16),
             vmem(act_inverse.shape, BF16),
-            vmem((feat, share), BF16),
+            vmem((n_row, feat, share), BF16),
             vmem((2, tok, samples), BF16),
             vmem((samples, feat), BF16),
-            vmem((3, 4, piece, share), F32),
-            vmem((3, 2, piece, share), BF16),
-            vmem((3, 2, piece, share), BF16),
-            vmem((3, piece, share), BF16),
-            vmem((3, piece, share), BF16),
+            vmem((2, 4, piece, share), F32),
+            vmem((2, 2, piece, share), BF16),
+            vmem((2, 2, piece, share), BF16),
+            vmem((2, piece, share), BF16),
+            vmem((2, piece, share), BF16),
+            vmem((4, 2, piece, share), F32),
+            vmem((4, piece, share), BF16),
+            vmem((4, piece, share), BF16),
+            vmem((4, piece, share), BF16),
+            vmem((4, piece, share), BF16),
             vmem((2, tok, out_rows), BF16),
             vmem((2, tok, out_rows), BF16),
             vmem((2, tok, out_rows), F32),
             vmem((tok, out_rows), BF16),
             vmem((tok, out_rows), BF16),
         ] + [vmem(s, BF16) for s in held] + [
-            pltpu.SemaphoreType.DMA((7,)),
+            pltpu.SemaphoreType.DMA((10,)),
             pltpu.SemaphoreType.DMA((9,)),
             pltpu.SemaphoreType.DMA((72,)),
             pltpu.SemaphoreType.DMA((72,)),
         ],
         compiler_params=pltpu.CompilerParams(
-            collective_id=0, has_side_effects=True, vmem_limit_bytes=60 * 2 ** 20
+            collective_id=0, has_side_effects=True, vmem_limit_bytes=58 * 2 ** 20
         ),
         cost_estimate=pl.CostEstimate(flops=3 * 10 ** 9, bytes_accessed=10 ** 7, transcendentals=0),
     )(rows, tokens_in, cotangent, act_inverse, grad_inverse)
@@ -405,7 +459,7 @@
             jax.ShapeDtypeStruct((xt.shape[0], xs.shape[1]), F32),
             jax.ShapeDtypeStruct((yt.shape[0], ys.shape[1]), F32),
         ],
-        compiler_params=pltpu.CompilerParams(vmem_limit_bytes=60 * 2 ** 20),
+        compiler_params=pltpu.CompilerParams(vmem_limit_bytes=40 * 2 ** 20),
         cost_estimate=pl.CostEstimate(flops=10 ** 9, bytes_accessed=17 * 10 ** 6, transcendentals=0),
     )(ut, v, xt, xs, yt, ys)
 

time: 43.6 us -> 40.9 us (0.938)
  Pallas kernels: 42.7 us -> 40.1 us
    pallas_call x1, Pallas kernels: 7.62 us -> 6.03 us  [products(): pl.pallas_call(functools.partial(product_kernel, total), grid=(steps,), i...]
    pallas_call x1, Pallas kernels: 35.1 us -> 34.1 us  [gather(): pl.pallas_call(gather_kernel, out_shape=[vmem(s, BF16) for s in shapes],...]
where the time goes in v6:
time: 40.9 us; the launch traced here: 40.8 us
  Pallas kernels  40.1 us (98%)
  between operations  0.64 us (2%)
    pallas_call x1, Pallas kernels, gather(): pl.pallas_call(gather_kernel, out_shape=[vmem(s, BF16) for s in shapes],...  34.1 us
    pallas_call x1, Pallas kernels, products(): pl.pallas_call(functools.partial(product_kernel, total), grid=(steps,), i...  6.03 us

profile of v6, /device:TPU:0, one launch (start us, length us, event | category | flops | bytes accessed | tf_op | source)
XLA Modules:
  0.0 40.8 jit_solution(13778927179505894940)
XLA Ops:
  0.6 34.1 %shard_map.76 = (bf16[384,256]{1,0:T(8,128)(2,1)S(1)}, bf16[256,3072]{1,0:T(8,128)(2,1)S(1)}, bf16[768,64]{1,0:T(8,128)(2,1)S(1)}, bf16[2,32,1536]{2,1,0:T(8,128...) custom-call(s32[1,32]{1,0:T(1,128)} %bitcast.5, bf16[128,1536]{1,0:T(8,128)(2,1)} %t_hbm.1, ...), custom_call_target="tpu_custom_call" | custom-call | flops 3000000000 | bytes 10000000 | tf_op jit(solution)/shard_map/pallas_call | solution.py:391
  34.7 6.0 %shard_map.77 = (f32[384,3072]{1,0:T(8,128)}, f32[768,1536]{1,0:T(8,128)}, f32[768,1536]{1,0:T(8,128)}) custom-call(bf16[384,256]{1,0:T(8,128)(2,1)S(1)} %get-tuple-element.9.ut, bf16[256,3072]{1,0:T(8,128)(2,1)S(1)} %get-tuple-element.10.v, bf16[768,64]{1,0:T(8,128)(2,1)S(1)} %get-tuple-element.11.xt, bf16[64,1536]{1,0:T(8,128)(2,1)S(1)} %bitcast.3, ...), custom_call_target="tpu_custom_call" | custom-call | flops 1000000000 | bytes 17000000 | tf_op jit(solution)/shard_map/pallas_call | solution.py:447

commit v7 on v5

--- a/solution.py
+++ b/solution.py
@@ -186,12 +186,15 @@
             got = v_v.at[rows_b(ph, ok), j * share:(j + 1) * share]
             await_in(("bk", 4 * (ph - 1) + j), got, to_k)
 
-    def run_b(ph):
-        product_b(ph, 0)
+    def run_b(ph, between=None):
+        for j in range(3):
+            product_b(ph, j)
+        across_b(ph, 0)
+        product_b(ph, 3)
+        if between:
+            between()
         for j in range(1, 4):
-            product_b(ph, j)
-            across_b(ph, j - 1)
-        across_b(ph, 3)
+            across_b(ph, j)
 
     def u_part(block):
         rows = a_v[pl.ds(pl.multiple_of(block * out_rows, out_rows), out_rows), :]
@@ -268,8 +271,7 @@
     spread(0, 1)
     spread(0, 2)
     await_cot(2)
-    run_b(2)
-    spread(0, 3)
+    run_b(2, lambda: spread(0, 3))
     for j in range(4):
         finish_b(1, j)
     send("xl", at_half(px_v, oc), xl_v.at[c], to_y)
@@ -375,7 +377,7 @@
     vmem = pltpu.VMEM
     return pl.pallas_call(
         gather_kernel,
-        out_shape=[jax.ShapeDtypeStruct(s, BF16) for s in shapes],
+        out_shape=[vmem(s, BF16) for s in shapes],
         in_specs=[pl.BlockSpec(memory_space=vmem)] + [pl.BlockSpec(memory_space=pl.ANY)] * 4,
         out_specs=[pl.BlockSpec(memory_space=pl.ANY)] * 6,
         scratch_shapes=[
@@ -407,7 +409,7 @@
             pltpu.SemaphoreType.DMA((72,)),
         ],
         compiler_params=pltpu.CompilerParams(
-            collective_id=0, has_side_effects=True, vmem_limit_bytes=60 * 2 ** 20
+            collective_id=0, has_side_effects=True, vmem_limit_bytes=58 * 2 ** 20
         ),
         cost_estimate=pl.CostEstimate(flops=3 * 10 ** 9, bytes_accessed=10 ** 7, transcendentals=0),
     )(rows, tokens_in, cotangent, act_inverse, grad_inverse)
@@ -444,7 +446,7 @@
             jax.ShapeDtypeStruct((xt.shape[0], xs.shape[1]), F32),
             jax.ShapeDtypeStruct((yt.shape[0], ys.shape[1]), F32),
         ],
-        compiler_params=pltpu.CompilerParams(vmem_limit_bytes=60 * 2 ** 20),
+        compiler_params=pltpu.CompilerParams(vmem_limit_bytes=40 * 2 ** 20),
         cost_estimate=pl.CostEstimate(flops=10 ** 9, bytes_accessed=17 * 10 ** 6, transcendentals=0),
     )(ut, v, xt, xs, yt, ys)
 

time: 40.2 us -> 38.4 us (0.955)
  Pallas kernels: 39.3 us -> 37.7 us
    pallas_call x1, Pallas kernels: 7.62 us -> 6.04 us  [products(): pl.pallas_call(functools.partial(product_kernel, total), grid=(steps,), i...]
where the time goes in v7:
time: 38.4 us; the launch traced here: 38.3 us
  Pallas kernels  37.7 us (98%)
  between operations  0.64 us (2%)
    pallas_call x1, Pallas kernels, gather(): pl.pallas_call(gather_kernel, out_shape=[vmem(s, BF16) for s in shapes],...  31.6 us
    pallas_call x1, Pallas kernels, products(): pl.pallas_call(functools.partial(product_kernel, total), grid=(steps,), i...  6.04 us

profile of v7, /device:TPU:0, one launch (start us, length us, event | category | flops | bytes accessed | tf_op | source)
XLA Modules:
  0.0 38.3 jit_solution(13468697532040913519)
XLA Ops:
  0.6 31.6 %shard_map.76 = (bf16[384,256]{1,0:T(8,128)(2,1)S(1)}, bf16[256,3072]{1,0:T(8,128)(2,1)S(1)}, bf16[768,64]{1,0:T(8,128)(2,1)S(1)}, bf16[2,32,1536]{2,1,0:T(8,128...) custom-call(s32[1,32]{1,0:T(1,128)} %bitcast.5, bf16[128,1536]{1,0:T(8,128)(2,1)} %t_hbm.1, ...), custom_call_target="tpu_custom_call" | custom-call | flops 3000000000 | bytes 10000000 | tf_op jit(solution)/shard_map/pallas_call | solution.py:378
  32.3 6.0 %shard_map.77 = (f32[384,3072]{1,0:T(8,128)}, f32[768,1536]{1,0:T(8,128)}, f32[768,1536]{1,0:T(8,128)}) custom-call(bf16[384,256]{1,0:T(8,128)(2,1)S(1)} %get-tuple-element.9.ut, bf16[256,3072]{1,0:T(8,128)(2,1)S(1)} %get-tuple-element.10.v, bf16[768,64]{1,0:T(8,128)(2,1)S(1)} %get-tuple-element.11.xt, bf16[64,1536]{1,0:T(8,128)(2,1)S(1)} %bitcast.3, ...), custom_call_target="tpu_custom_call" | custom-call | flops 1000000000 | bytes 17000000 | tf_op jit(solution)/shard_map/pallas_call | solution.py:434

commit v8 on v7

--- a/solution.py
+++ b/solution.py
@@ -87,9 +87,11 @@
         pl.semaphore_signal(barrier, inc=1, device_id=where, device_id_type=pl.DeviceIdType.MESH)
     pl.semaphore_wait(barrier, len(partners))
 
-    for ph in (1, 2):
+    def send_cot(ph):
         part = pl.ds(phases[ph][1], phases[ph][2])
         send(("cot", ph), c_hbm.at[part], c_v.at[c, part], to_y)
+
+    send_cot(1)
 
     hot = lax.broadcasted_iota(jnp.int32, (tok, rows_ref.shape[1]), 0) + c * tok == rows_ref[...]
     oh_v[c] = jnp.where(hot, 1.0, 0.0).astype(BF16)
@@ -228,6 +230,7 @@
         loads[1 + i].wait()
         w_s[i] = u_part(away_blocks[i]).astype(BF16)
     send("w", w_s, w_r, to_z1)
+    send_cot(2)
     loads[3].wait()
     loads[4].wait()
     product(0)

time: 38.4 us -> 38.4 us (level)
  no operation moved by 1% of the time
where the time goes in v8:
time: 38.4 us; the launch traced here: 38.3 us
  Pallas kernels  37.7 us (98%)
  between operations  0.64 us (2%)
    pallas_call x1, Pallas kernels, gather(): pl.pallas_call(gather_kernel, out_shape=[vmem(s, BF16) for s in shapes],...  31.6 us
    pallas_call x1, Pallas kernels, products(): pl.pallas_call(functools.partial(product_kernel, total), grid=(steps,), i...  6.03 us

profile of v8, /device:TPU:0, one launch (start us, length us, event | category | flops | bytes accessed | tf_op | source)
XLA Modules:
  0.0 38.3 jit_solution(11302098291138395318)
XLA Ops:
  0.6 31.6 %shard_map.76 = (bf16[384,256]{1,0:T(8,128)(2,1)S(1)}, bf16[256,3072]{1,0:T(8,128)(2,1)S(1)}, bf16[768,64]{1,0:T(8,128)(2,1)S(1)}, bf16[2,32,1536]{2,1,0:T(8,128...) custom-call(s32[1,32]{1,0:T(1,128)} %bitcast.5, bf16[128,1536]{1,0:T(8,128)(2,1)} %t_hbm.1, ...), custom_call_target="tpu_custom_call" | custom-call | flops 3000000000 | bytes 10000000 | tf_op jit(solution)/shard_map/pallas_call | solution.py:381
  32.3 6.0 %shard_map.77 = (f32[384,3072]{1,0:T(8,128)}, f32[768,1536]{1,0:T(8,128)}, f32[768,1536]{1,0:T(8,128)}) custom-call(bf16[384,256]{1,0:T(8,128)(2,1)S(1)} %get-tuple-element.9.ut, bf16[256,3072]{1,0:T(8,128)(2,1)S(1)} %get-tuple-element.10.v, bf16[768,64]{1,0:T(8,128)(2,1)S(1)} %get-tuple-element.11.xt, bf16[64,1536]{1,0:T(8,128)(2,1)S(1)} %bitcast.3, ...), custom_call_target="tpu_custom_call" | custom-call | flops 1000000000 | bytes 17000000 | tf_op jit(solution)/shard_map/pallas_call | solution.py:437
